TPU v7x, 32 devices: a whole 2x2x4 slice. The times are simulated.
32 devices in a mesh: seq: 8 (over z, y), mp: 4 (over x, core).
Axes of the slice: x: 2, y: 2, z: 4, core: 2. Of those that a mesh axis runs over, the one named last changes fastest.
Arguments:
- tokens: bfloat16 [2304, 1536], P('seq'), may hold values from -6 to 6
- norm_gain: float32 [1536], replicated, may hold values from 0.5 to 1.5
- w_query: bfloat16 [1536, 1536], P(None, 'mp')
- w_key: bfloat16 [1536, 1536], P(None, 'mp')
- w_value: bfloat16 [1536, 1536], P(None, 'mp'), may hold values from -0.15625 to 0.15625
- w_out: bfloat16 [1536, 1536], P('mp'), may hold values from -0.15625 to 0.15625
- w_shorten: bfloat16 [13824, 1536], P('seq', 'mp'), may hold values from -0.0546875 to 0.0546875
- first_key: int32 [256], P('seq'), may hold values from 0 to 2295, as said below
- d_faces: bfloat16 [256, 1536], P('seq', 'mp'), may hold values from -6 to 6
Outputs:
- faces: bfloat16 [256, 1536], P('seq', 'mp')
- d_tokens: bfloat16 [2304, 1536], P('seq')
Inputs may be any that keep to these rules, and one draw needn't show every extreme that they name: first_key is a multiple of 9, never above the position of its face's first token, never decreases from one face to the next, and equals that position at every face where a new mesh begins; face 0 and the last face begin meshes.
All inputs are finite; a program needn't handle non-finite values.
Results may differ from a plain program's by a relative error of at most 0.014.
Values may be sent and summed in bfloat16 or wider, within the bound.
A program may use at most 128 MiB of HBM per device.

v0:
```python
import jax
import jax.numpy as jnp
from jax import lax
from jax.sharding import PartitionSpec as P

HEAD = 64
WIN = 4096


def shifted(array, axis, by):
    size = lax.axis_size(axis)
    pairs = [(i, i + by) for i in range(size) if 0 <= i + by < size]
    return lax.ppermute(array, axis, pairs)


def shortened(array):

    def short(part):
        return part.astype(jnp.bfloat16) if part.dtype == jnp.float32 else part

    return jax.tree.map(short, array)


def times_rows(left, right):
    return lax.dot_general(
        left, right, (((1,), (1,)), ((), ())), preferred_element_type=jnp.float32
    )


def times_cols(left, right):
    return lax.dot_general(
        left, right, (((0,), (0,)), ((), ())), preferred_element_type=jnp.float32
    )


def finish(d_normed, x_float, scale_r, d_mixed, norm_gain):
    inner_sum = jnp.mean(d_normed * norm_gain * x_float, axis=-1, keepdims=True)
    return (
        d_mixed.astype(jnp.float32)
        + scale_r * norm_gain * d_normed
        - x_float * scale_r**3 * inner_sum
    )


def local(tokens, norm_gain, w_query, w_key, w_value, w_out, w_shorten, first_key, d_faces):
    tok_rows = tokens.shape[0]
    model_width = tokens.shape[1]
    face_rows = tok_rows // 9
    local_width = w_query.shape[1]
    local_heads = local_width // HEAD
    seq_count = lax.axis_size("seq")
    hops = min(-(-WIN // tok_rows), seq_count - 1)
    levels = hops.bit_length()
    seq_index = lax.axis_index("seq")
    x_float = tokens.astype(jnp.float32)
    scale_r = lax.rsqrt(jnp.mean(x_float * x_float, axis=-1, keepdims=True) + 1e-05)
    normed = (x_float * scale_r * norm_gain).astype(jnp.bfloat16)
    query = jnp.dot(normed, w_query, preferred_element_type=jnp.float32).astype(jnp.bfloat16)
    key = jnp.dot(normed, w_key, preferred_element_type=jnp.float32).astype(jnp.bfloat16)
    value = jnp.dot(normed, w_value, preferred_element_type=jnp.float32).astype(jnp.bfloat16)
    stacked_key = key[None]
    stacked_value = value[None]
    for level in range(levels):
        reach_by = 1 << level
        came_key, came_value = shifted((stacked_key, stacked_value), "seq", reach_by)
        stacked_key = jnp.concatenate([stacked_key, came_key], axis=0)
        stacked_value = jnp.concatenate([stacked_value, came_value], axis=0)
    anchors = seq_index - jnp.arange(hops + 1, dtype=jnp.int32)
    block_count = stacked_key.shape[0]
    key_total = block_count * tok_rows
    pos_q = seq_index * tok_rows + jnp.arange(tok_rows, dtype=jnp.int32)
    pos_k = (anchors[:, None] * tok_rows + jnp.arange(tok_rows, dtype=jnp.int32)[None, :]).reshape(
        key_total
    )
    lower_bound = jnp.repeat(first_key, 9)
    allowed = (
        (pos_k[None, :] >= lower_bound[:, None])
        & (pos_k[None, :] <= pos_q[:, None])
        & (pos_q[:, None] - pos_k[None, :] < WIN)
    )
    query_heads = query.reshape(tok_rows, local_heads, HEAD).transpose(1, 0, 2)
    key_heads = stacked_key.reshape(key_total, local_heads, HEAD).transpose(1, 0, 2)
    value_heads = stacked_value.reshape(key_total, local_heads, HEAD).transpose(1, 0, 2)

    def head_probs(query_head, key_head):
        scores = times_rows(query_head, key_head) * HEAD ** (-0.5)
        scores = jnp.where(allowed, scores, -1e30)
        row_top = jnp.max(scores, axis=-1, keepdims=True)
        raised = jnp.exp(scores - row_top)
        return raised / jnp.sum(raised, axis=-1, keepdims=True)

    def head_forward(operands):
        query_head, key_head, value_head = operands
        probs = head_probs(query_head, key_head)
        return jnp.dot(
            probs.astype(jnp.bfloat16), value_head, preferred_element_type=jnp.float32
        ).astype(jnp.bfloat16)

    att_heads = lax.map(head_forward, (query_heads, key_heads, value_heads))
    attended = att_heads.transpose(1, 0, 2).reshape(tok_rows, local_width)
    projected = jnp.dot(attended, w_out, preferred_element_type=jnp.float32)
    summed = lax.psum(projected.astype(jnp.bfloat16), "mp").astype(jnp.float32)
    mixed = (x_float + summed).astype(jnp.bfloat16)
    mixed_faces = mixed.reshape(face_rows, 9 * model_width)
    full_shorten = lax.all_gather(w_shorten, "seq", axis=0, tiled=True)
    face_sum = jnp.dot(mixed_faces, full_shorten, preferred_element_type=jnp.float32)
    d_partial = times_rows(d_faces, full_shorten)
    faces = face_sum.astype(jnp.bfloat16)
    d_mixed = lax.psum(d_partial, "mp").astype(jnp.bfloat16).reshape(tok_rows, model_width)
    d_attended = times_rows(d_mixed, w_out).astype(jnp.bfloat16)
    d_att_heads = d_attended.reshape(tok_rows, local_heads, HEAD).transpose(1, 0, 2)

    def head_backward(operands):
        query_head, key_head, value_head, d_att_head, att_head = operands
        probs = head_probs(query_head, key_head)
        d_probs = times_rows(d_att_head, value_head)
        row_delta = jnp.sum(d_att_head.astype(jnp.float32) * att_head.astype(jnp.float32), axis=-1)
        d_scores = (probs * (d_probs - row_delta[:, None])).astype(jnp.bfloat16)
        d_query_head = (
            jnp.dot(d_scores, key_head, preferred_element_type=jnp.float32) * HEAD ** (-0.5)
        ).astype(jnp.bfloat16)
        d_key_head = times_cols(d_scores, query_head) * HEAD ** (-0.5)
        d_value_head = times_cols(probs.astype(jnp.bfloat16), d_att_head)
        return (d_query_head, d_key_head, d_value_head)

    d_query_heads, d_key_heads, d_value_heads = lax.map(
        head_backward, (query_heads, key_heads, value_heads, d_att_heads, att_heads)
    )
    d_query = d_query_heads.transpose(1, 0, 2).reshape(tok_rows, local_width)
    d_key_parts = d_key_heads.transpose(1, 0, 2).reshape(block_count, tok_rows, local_width)
    d_value_parts = d_value_heads.transpose(1, 0, 2).reshape(block_count, tok_rows, local_width)
    spare_blocks = (1 << levels) - block_count
    filler = jnp.zeros((spare_blocks, tok_rows, local_width), jnp.float32)
    parts_key = jnp.concatenate([d_key_parts, filler], axis=0)
    parts_value = jnp.concatenate([d_value_parts, filler], axis=0)
    for level in reversed(range(levels)):
        reach_by = 1 << level
        came_key, came_value = shifted(
            (
                shortened(parts_key[reach_by : 2 * reach_by]),
                shortened(parts_value[reach_by : 2 * reach_by]),
            ),
            "seq",
            -reach_by,
        )
        parts_key = parts_key[:reach_by] + came_key
        parts_value = parts_value[:reach_by] + came_value
    acc_key, acc_value = (parts_key[0], parts_value[0])
    d_key = acc_key.astype(jnp.bfloat16)
    d_value = acc_value.astype(jnp.bfloat16)
    part_normed = times_rows(d_query, w_query)
    part_normed = part_normed + times_rows(d_key, w_key)
    part_normed = part_normed + times_rows(d_value, w_value)
    d_normed = lax.psum(part_normed.astype(jnp.bfloat16), "mp").astype(jnp.float32)
    d_tokens = finish(d_normed, x_float, scale_r, d_mixed, norm_gain).astype(jnp.bfloat16)
    return (faces, d_tokens)


def solution(mesh):
    in_specs = (
        P("seq", None),
        P(),
        P(None, "mp"),
        P(None, "mp"),
        P(None, "mp"),
        P("mp", None),
        P("seq", "mp"),
        P("seq"),
        P("seq", "mp"),
    )
    out_specs = (P("seq", "mp"), P("seq", None))
    return jax.shard_map(local, mesh=mesh, in_specs=in_specs, out_specs=out_specs, check_vma=False)
```

profile of v0, /device:TPU:0, one launch (start us, length us, event | category | flops | bytes accessed | tf_op | source)
XLA Modules:
  0.0 543.5 jit_solution(9463587554302113907)
XLA Ops:
  10.8 4.9 collective-permute-start.3
  16.4 3.4 collective-permute-start
  21.2 5.4 collective-permute-start.4
  29.5 5.4 %collective-permute-start.1 = (bf16[2,288,384]{2,1,0:T(8,128)(2,1)}, bf16[2,288,384]{2,1,0:T(8,128)(2,1)S(1)}, u32[]{:S(2)}, u32[]{:S(2)}) collective-permute-start(bf16[2,288,384]{2,1,0:T(8,128)(2,1)} %pad_maximum_fusion.4), channel_id=1, source_target_pairs={{0,8},{4,12},{8,16},{12,20},{16,24},{20,28},{1,9},{5,13},{9,17},{1... | collective-permute-start | bytes 1327112 | tf_op jit(solution)/shard_map/ppermute | solution.py:13
  34.9 11.6 %collective-permute-done.4 = bf16[2,288,384]{2,1,0:T(8,128)(2,1)S(1)} collective-permute-done((bf16[2,288,384]{2,1,0:T(8,128)(2,1)S(1)}, bf16[2,288,384]{2,1,0:T(8,128)(2,1)S(1)}, u32[]{:S(2)}, u32[]{:S(2)}) %collective-permute-start.4) | collective-permute-done | bytes 442400 | tf_op jit(solution)/shard_map/ppermute | solution.py:13
  48.3 15.8 %collective-permute-start.5 = (bf16[4,288,384]{2,1,0:T(8,128)(2,1)}, bf16[4,288,384]{2,1,0:T(8,128)(2,1)}, u32[]{:S(2)}, u32[]{:S(2)}) collective-permute-start(bf16[4,288,384]{2,1,0:T(8,128)(2,1)} %pad_maximum_fusion.3), channel_id=1, source_target_pairs={{0,16},{4,20},{8,24},{12,28},{1,17},{5,21},{9,25},{13,29},{2,18},{... | collective-permute-start | bytes 2654216 | tf_op jit(solution)/shard_map/ppermute | solution.py:13
  66.7 53.9 %collective-permute-start.2 = (bf16[4,288,384]{2,1,0:T(8,128)(2,1)}, bf16[4,288,384]{2,1,0:T(8,128)(2,1)}, u32[]{:S(2)}, u32[]{:S(2)}) collective-permute-start(bf16[4,288,384]{2,1,0:T(8,128)(2,1)} %pad_maximum_fusion.2), channel_id=1, source_target_pairs={{0,16},{4,20},{8,24},{12,28},{1,17},{5,21},{9,25},{13,29},{2,18},{... | collective-permute-start | bytes 2654216 | tf_op jit(solution)/shard_map/ppermute | solution.py:13
  120.6 3.0 convolution_convert_fusion.4
  127.8 2.6 pad_maximum_fusion.1
  130.4 3.2 copy.58
  133.6 2.9 reshape.91
  136.5 4.6 copy.61
  141.2 8.2 %collective-permute-done.2 = bf16[4,288,384]{2,1,0:T(8,128)(2,1)} collective-permute-done((bf16[4,288,384]{2,1,0:T(8,128)(2,1)}, bf16[4,288,384]{2,1,0:T(8,128)(2,1)}, u32[]{:S(2)}, u32[]{:S(2)}) %collective-permute-start.2) | collective-permute-done | bytes 884768 | tf_op jit(solution)/shard_map/ppermute | solution.py:13
  149.4 2.6 pad_maximum_fusion
  152.0 3.2 copy.57
  155.2 2.9 reshape.90
  158.2 4.6 copy.60
  162.8 27.4 %while.26 = (s32[]{:T(128)}, bf16[6,288,64]{1,2,0:T(8,128)(2,1)S(1)}, bf16[6,288,64]{2,1,0:T(8,128)(2,1)}, bf16[6,2304,64]{2,1,0:T(8,128)(2,1)}, bf16[6,2304,64]...) while((s32[]{:T(128)}, ...), condition=%wide.region_4.5_spmd.clone, body=%wide.region_1.4_spmd.clone.sunk | while | flops 179176896 | bytes 9286365 | solution.py:99
  167.4 2.2 fusion.112
  181.1 2.3 fusion.112
  190.2 26.0 %all-gather.2.cloned.1.call-done = bf16[13824,384]{1,0:T(8,128)(2,1)} async-done(((bf16[1728,384]{1,0:T(8,128)(2,1)}), bf16[13824,384]{1,0:T(8,128)(2,1)}) %all-gather.2.cloned.1.call-update) | async-done | bytes 10616848 | tf_op jit(solution)/shard_map/all_gather | solution.py:105
  216.3 7.4 %fusion.73 = f32[32,13824]{1,0:T(8,128)S(1)} fusion(bf16[32,384]{1,0:T(8,128)(2,1)S(1)} %copy-done.24, bf16[13824,384]{1,0:T(8,128)(2,1)} %all-gather.2.cloned.1.call-done), kind=kOutput, calls=%fused_computation.118 | convolution fusion | flops 339738624 | bytes 12410880 | tf_op jit(solution)/shard_map/dot_general | solution.py:25
  223.6 36.7 %all-reduce.5 = bf16[32,13824]{1,0:T(8,128)(2,1)} all-reduce(f32[32,13824]{1,0:T(8,128)S(1)} %fusion.73), channel_id=1, replica_groups=mesh['seq'=8,'mp'=4] {'mp'}, use_global_device_ids=true, to_apply=%region_6.7 | all-reduce | flops 442368 | bytes 2654208 | tf_op jit(solution)/shard_map/psum | solution.py:109
  260.3 2.5 reshape.94
  263.7 68.0 %while.27 = (s32[]{:T(128)}, bf16[6,288,64]{1,2,0:T(8,128)(2,1)S(1)}, f32[6,2304,64]{1,2,0:T(8,128)}, f32[6,2304,64]{1,2,0:T(8,128)}, bf16[6,288,64]{2,1,0:T(8,1...) while((s32[]{:T(128)}, ...), condition=%wide.region_11.12_spmd.clone, body=%wide.region_7.11_spmd.clone.sunk | while | flops 437537952 | bytes 28859292 | solution.py:126
  268.4 2.8 fusion.126
  279.7 2.9 fusion.126
  282.6 2.2 fusion.128
  286.4 2.2 fusion.124
  291.1 2.8 fusion.126
  297.8 2.2 fusion.124
  302.4 2.8 fusion.126
  309.1 2.2 fusion.124
  313.7 2.8 fusion.126
  325.1 2.8 fusion.126
  346.1 2.8 slice.70
  348.9 2.8 slice.64
  351.8 2.8 slice.58
  354.6 2.4 copy.71
  357.0 2.8 slice.51
  359.8 2.5 copy.69
  362.3 20.9 %collective-permute-done.6 = bf16[4,288,384]{2,1,0:T(8,128)(2,1)} collective-permute-done((bf16[4,288,384]{2,1,0:T(8,128)(2,1)}, bf16[4,288,384]{2,1,0:T(8,128)(2,1)}, u32[]{:S(2)}, u32[]{:S(2)}) %collective-permute-start.6) | collective-permute-done | bytes 884768 | tf_op jit(solution)/shard_map/ppermute | solution.py:13
  386.6 53.5 %collective-permute-done.9 = bf16[4,288,384]{2,1,0:T(8,128)(2,1)} collective-permute-done((bf16[4,288,384]{2,1,0:T(8,128)(2,1)}, bf16[4,288,384]{2,1,0:T(8,128)(2,1)}, u32[]{:S(2)}, u32[]{:S(2)}) %collective-permute-start.9) | collective-permute-done | bytes 884768 | tf_op jit(solution)/shard_map/ppermute | solution.py:13
  445.1 11.4 %collective-permute-done.10 = bf16[2,288,384]{2,1,0:T(8,128)(2,1)S(1)} collective-permute-done((bf16[2,288,384]{2,1,0:T(8,128)(2,1)S(1)}, bf16[2,288,384]{2,1,0:T(8,128)(2,1)S(1)}, u32[]{:S(2)}, u32[]{:S(2)}) %collective-permute-start.10) | collective-permute-done | bytes 442400 | tf_op jit(solution)/shard_map/ppermute | solution.py:13
  458.8 11.2 %collective-permute-done.11 = bf16[1,288,384]{2,1,0:T(8,128)(2,1)S(1)} collective-permute-done((bf16[1,288,384]{2,1,0:T(8,128)(2,1)S(1)}, bf16[1,288,384]{2,1,0:T(8,128)(2,1)S(1)}, u32[]{:S(2)}, u32[]{:S(2)}) %collective-permute-start.11) | collective-permute-done | bytes 221216 | tf_op jit(solution)/shard_map/ppermute | solution.py:13
  471.7 52.6 %all-reduce.4.cloned.1.call-done = (bf16[288,1536]{1,0:T(8,128)(2,1)}, bf16[288,1536]{1,0:T(8,128)(2,1)}) async-done(((bf16[288,1536]{1,0:T(8,128)(2,1)}, bf16[288,1536]{1,0:T(8,128)(2,1)}), (bf16[288,1536]{1,0:T(8,128)(2,1)}, bf16[288,1536]{1,0:T(8,128)(2,1)})) %all-reduce.4.cloned.1.call-update) | async-done | bytes 1769488 | tf_op jit(solution)/shard_map/psum | solution.py:102
  527.9 2.5 reshape.93
  530.4 6.3 %convolution_convert_fusion.5 = bf16[32,384]{1,0:T(8,128)(2,1)} fusion(bf16[32,13824]{1,0:T(8,128)(2,1)S(1)} %reshape.93, bf16[13824,384]{1,0:T(8,128)(2,1)} %all-gather.2.cloned.1.call-done), kind=kOutput, calls=%fused_computation.93 | convolution fusion | flops 339750912 | bytes 11526144 | tf_op jit(solution)/shard_map/dot_general | solution.py:106
  (193 shorter events, 112.8 us)
Async XLA Ops:
  7.2 255.6 %copy-start = (bf16[384,1536]{1,0:T(8,128)(2,1)S(1)}, bf16[384,1536]{1,0:T(8,128)(2,1)}, u32[]{:S(2)}) copy-start(bf16[384,1536]{1,0:T(8,128)(2,1)} %param.18) | copy-start | bytes 3538948
  7.2 1.3 copy-start.2
  7.2 1.5 copy-start.23
  7.2 209.1 %all-gather.2.cloned.1.call-start = ((), (), s32[]{:S(2)}) async-start(), calls=%async_computation | async-start | bytes 11943936 | tf_op jit(solution)/shard_map/all_gather | solution.py:105
  7.9 516.3 %all-reduce.4.cloned.1.call-start = ((), (), s32[]{:S(2)}) async-start(), calls=%async_computation.1 | async-start | bytes 3538944 | tf_op jit(solution)/shard_map/psum | solution.py:102
  8.7 7.0 %copy-start.19 = (bf16[1536,384]{1,0:T(8,128)(2,1)S(1)}, bf16[1536,384]{1,0:T(8,128)(2,1)}, u32[]{:S(2)}) copy-start(bf16[1536,384]{1,0:T(8,128)(2,1)} %param.16) | copy-start | bytes 3538948
  10.8 10.4 %collective-permute-start.3 = (bf16[1,288,384]{2,1,0:T(8,128)(2,1)S(1)}, bf16[1,288,384]{2,1,0:T(8,128)(2,1)S(1)}, u32[]{:S(2)}, u32[]{:S(2)}) collective-permute-start(bf16[1,288,384]{2,1,0:T(8,128)(2,1)S(1)} %fusion.61), channel_id=1, source_target_pairs={{0,4},{4,8},{8,12},{12,16},{16,20},{20,24},{24,28},{1,5},{5,9},{9,... | collective-permute-start | bytes 663560 | tf_op jit(solution)/shard_map/ppermute | solution.py:13
  16.4 49.2 %copy-start.8 = (bf16[1,288,384]{2,1,0:T(8,128)(2,1)}, bf16[1,288,384]{2,1,0:T(8,128)(2,1)S(1)}, u32[]{:S(2)}) copy-start(bf16[1,288,384]{2,1,0:T(8,128)(2,1)S(1)} %fusion.60) | copy-start | bytes 663556
  16.4 12.3 %collective-permute-start = (bf16[1,288,384]{2,1,0:T(8,128)(2,1)S(1)}, bf16[1,288,384]{2,1,0:T(8,128)(2,1)S(1)}, u32[]{:S(2)}, u32[]{:S(2)}) collective-permute-start(bf16[1,288,384]{2,1,0:T(8,128)(2,1)S(1)} %fusion.60), channel_id=1, source_target_pairs={{0,4},{4,8},{8,12},{12,16},{16,20},{20,24},{24,28},{1,5},{5,9},{9,... | collective-permute-start | bytes 663560 | tf_op jit(solution)/shard_map/ppermute | solution.py:13
  21.2 25.3 %collective-permute-start.4 = (bf16[2,288,384]{2,1,0:T(8,128)(2,1)S(1)}, bf16[2,288,384]{2,1,0:T(8,128)(2,1)S(1)}, u32[]{:S(2)}, u32[]{:S(2)}) collective-permute-start(bf16[2,288,384]{2,1,0:T(8,128)(2,1)S(1)} %pad_maximum_fusion.5), channel_id=1, source_target_pairs={{0,8},{4,12},{8,16},{12,20},{16,24},{20,28},{1,9},{5,13},{9,17},{1... | collective-permute-start | bytes 1327112 | tf_op jit(solution)/shard_map/ppermute | solution.py:13
  28.6 38.0 %copy-start.10 = (bf16[1,288,384]{2,1,0:T(8,128)(2,1)}, bf16[1,288,384]{2,1,0:T(8,128)(2,1)S(1)}, u32[]{:S(2)}) copy-start(bf16[1,288,384]{2,1,0:T(8,128)(2,1)S(1)} %collective-permute-done) | copy-start | bytes 663556
  29.5 36.1 %collective-permute-start.1 = (bf16[2,288,384]{2,1,0:T(8,128)(2,1)}, bf16[2,288,384]{2,1,0:T(8,128)(2,1)S(1)}, u32[]{:S(2)}, u32[]{:S(2)}) collective-permute-start(bf16[2,288,384]{2,1,0:T(8,128)(2,1)} %pad_maximum_fusion.4), channel_id=1, source_target_pairs={{0,8},{4,12},{8,16},{12,20},{16,24},{20,28},{1,9},{5,13},{9,17},{1... | collective-permute-start | bytes 1327112 | tf_op jit(solution)/shard_map/ppermute | solution.py:13
  46.5 0.8 copy-start.14
  48.3 79.5 %collective-permute-start.5 = (bf16[4,288,384]{2,1,0:T(8,128)(2,1)}, bf16[4,288,384]{2,1,0:T(8,128)(2,1)}, u32[]{:S(2)}, u32[]{:S(2)}) collective-permute-start(bf16[4,288,384]{2,1,0:T(8,128)(2,1)} %pad_maximum_fusion.3), channel_id=1, source_target_pairs={{0,16},{4,20},{8,24},{12,28},{1,17},{5,21},{9,25},{13,29},{2,18},{... | collective-permute-start | bytes 2654216 | tf_op jit(solution)/shard_map/ppermute | solution.py:13
  65.6 58.0 %copy-start.12 = (bf16[2,288,384]{2,1,0:T(8,128)(2,1)}, bf16[2,288,384]{2,1,0:T(8,128)(2,1)S(1)}, u32[]{:S(2)}) copy-start(bf16[2,288,384]{2,1,0:T(8,128)(2,1)S(1)} %collective-permute-done.1) | copy-start | bytes 1327108
  66.7 59.9 %copy-start.28 = (s32[32]{0:T(128)S(1)}, s32[32]{0:T(128)}, u32[]{:S(2)}) copy-start(s32[32]{0:T(128)} %param.20) | copy-start | bytes 388
  66.7 82.7 %collective-permute-start.2 = (bf16[4,288,384]{2,1,0:T(8,128)(2,1)}, bf16[4,288,384]{2,1,0:T(8,128)(2,1)}, u32[]{:S(2)}, u32[]{:S(2)}) collective-permute-start(bf16[4,288,384]{2,1,0:T(8,128)(2,1)} %pad_maximum_fusion.2), channel_id=1, source_target_pairs={{0,16},{4,20},{8,24},{12,28},{1,17},{5,21},{9,25},{13,29},{2,18},{... | collective-permute-start | bytes 2654216 | tf_op jit(solution)/shard_map/ppermute | solution.py:13
  120.6 7.3 %copy-start.15 = (bf16[2,288,384]{2,1,0:T(8,128)(2,1)S(1)}, bf16[2,288,384]{2,1,0:T(8,128)(2,1)}, u32[]{:S(2)}) copy-start(bf16[2,288,384]{2,1,0:T(8,128)(2,1)} %copy-done.14) | copy-start | bytes 1327108
  136.5 12.9 %copy-start.9 = (bf16[1,288,384]{2,1,0:T(8,128)(2,1)S(1)}, bf16[1,288,384]{2,1,0:T(8,128)(2,1)}, u32[]{:S(2)}) copy-start(bf16[1,288,384]{2,1,0:T(8,128)(2,1)} %copy-done.8) | copy-start | bytes 663556
  136.5 12.9 %copy-start.11 = (bf16[1,288,384]{2,1,0:T(8,128)(2,1)S(1)}, bf16[1,288,384]{2,1,0:T(8,128)(2,1)}, u32[]{:S(2)}) copy-start(bf16[1,288,384]{2,1,0:T(8,128)(2,1)} %copy-done.10) | copy-start | bytes 663556
  136.5 12.9 %copy-start.13 = (bf16[2,288,384]{2,1,0:T(8,128)(2,1)S(1)}, bf16[2,288,384]{2,1,0:T(8,128)(2,1)}, u32[]{:S(2)}) copy-start(bf16[2,288,384]{2,1,0:T(8,128)(2,1)} %copy-done.12) | copy-start | bytes 1327108
  158.2 4.6 copy-start.25
  158.2 4.6 copy-start.26
  158.2 4.6 copy-start.27
  162.8 53.5 %copy-start.24 = (bf16[32,384]{1,0:T(8,128)(2,1)S(1)}, bf16[32,384]{1,0:T(8,128)(2,1)}, u32[]{:S(2)}) copy-start(bf16[32,384]{1,0:T(8,128)(2,1)} %param.21) | copy-start | bytes 73732
  262.8 0.9 copy-start.5
  265.9 2.0 copy-start.1
  277.3 2.0 copy-start.1
  288.6 2.0 copy-start.1
  300.0 2.0 copy-start.1
  311.3 2.0 copy-start.1
  322.6 2.0 copy-start.1
  331.7 0.7 copy-start.16
  337.1 46.1 %collective-permute-start.6 = (bf16[4,288,384]{2,1,0:T(8,128)(2,1)}, bf16[4,288,384]{2,1,0:T(8,128)(2,1)}, u32[]{:S(2)}, u32[]{:S(2)}) collective-permute-start(bf16[4,288,384]{2,1,0:T(8,128)(2,1)} %copy.68), channel_id=1, source_target_pairs={{16,0},{20,4},{24,8},{28,12},{17,1},{21,5},{25,9},{29,13},{18,2},{... | collective-permute-start | bytes 2654216 | tf_op jit(solution)/shard_map/ppermute | solution.py:13
  343.0 97.0 %collective-permute-start.9 = (bf16[4,288,384]{2,1,0:T(8,128)(2,1)}, bf16[4,288,384]{2,1,0:T(8,128)(2,1)}, u32[]{:S(2)}, u32[]{:S(2)}) collective-permute-start(bf16[4,288,384]{2,1,0:T(8,128)(2,1)} %copy.70), channel_id=1, source_target_pairs={{16,0},{20,4},{24,8},{28,12},{17,1},{21,5},{25,9},{29,13},{18,2},{... | collective-permute-start | bytes 2654216 | tf_op jit(solution)/shard_map/ppermute | solution.py:13
  362.3 77.8 %copy-start.4 = (f32[4,288,384]{2,1,0:T(8,128)S(1)}, f32[4,288,384]{2,1,0:T(8,128)}, u32[]{:S(2)}) copy-start(f32[4,288,384]{2,1,0:T(8,128)} %copy.71) | copy-start | bytes 5308420
  385.1 57.7 %copy-start.17 = (bf16[6,288,64]{1,2,0:T(8,128)(2,1)S(1)}, bf16[6,288,64]{1,2,0:T(8,128)(2,1)}, u32[]{:S(2)}) copy-start(bf16[6,288,64]{1,2,0:T(8,128)(2,1)} %copy-done.16) | copy-start | bytes 663556
  385.1 57.7 %copy-start.18 = (bf16[1536,384]{1,0:T(8,128)(2,1)S(1)}, bf16[1536,384]{1,0:T(8,128)(2,1)}, u32[]{:S(2)}) copy-start(bf16[1536,384]{1,0:T(8,128)(2,1)} %param.15) | copy-start | bytes 3538948
  385.1 58.4 %collective-permute-start.7 = (bf16[2,288,384]{2,1,0:T(8,128)(2,1)S(1)}, bf16[2,288,384]{2,1,0:T(8,128)(2,1)S(1)}, u32[]{:S(2)}, u32[]{:S(2)}) collective-permute-start(bf16[2,288,384]{2,1,0:T(8,128)(2,1)S(1)} %slice.99), channel_id=1, source_target_pairs={{8,0},{12,4},{16,8},{20,12},{24,16},{28,20},{9,1},{13,5},{17,9},{2... | collective-permute-start | bytes 1327112 | tf_op jit(solution)/shard_map/ppermute | solution.py:13
  441.5 15.0 %collective-permute-start.10 = (bf16[2,288,384]{2,1,0:T(8,128)(2,1)S(1)}, bf16[2,288,384]{2,1,0:T(8,128)(2,1)S(1)}, u32[]{:S(2)}, u32[]{:S(2)}) collective-permute-start(bf16[2,288,384]{2,1,0:T(8,128)(2,1)S(1)} %slice.98), channel_id=1, source_target_pairs={{8,0},{12,4},{16,8},{20,12},{24,16},{28,20},{9,1},{13,5},{17,9},{2... | collective-permute-start | bytes 1327112 | tf_op jit(solution)/shard_map/ppermute | solution.py:13
  443.7 14.5 %copy-start.20 = (bf16[1536,384]{1,0:T(8,128)(2,1)S(1)}, bf16[1536,384]{1,0:T(8,128)(2,1)}, u32[]{:S(2)}) copy-start(bf16[1536,384]{1,0:T(8,128)(2,1)} %param.16) | copy-start | bytes 3538948
  443.7 14.4 %collective-permute-start.8 = (bf16[1,288,384]{2,1,0:T(8,128)(2,1)S(1)}, bf16[1,288,384]{2,1,0:T(8,128)(2,1)S(1)}, u32[]{:S(2)}, u32[]{:S(2)}) collective-permute-start(bf16[1,288,384]{2,1,0:T(8,128)(2,1)S(1)} %slice.101), channel_id=1, source_target_pairs={{4,0},{8,4},{12,8},{16,12},{20,16},{24,20},{28,24},{5,1},{9,5},{13... | collective-permute-start | bytes 663560 | tf_op jit(solution)/shard_map/ppermute | solution.py:13
  456.7 13.3 %copy-start.21 = (bf16[1536,384]{1,0:T(8,128)(2,1)S(1)}, bf16[1536,384]{1,0:T(8,128)(2,1)}, u32[]{:S(2)}) copy-start(bf16[1536,384]{1,0:T(8,128)(2,1)} %param.17) | copy-start | bytes 3538948
  456.7 13.3 %collective-permute-start.11 = (bf16[1,288,384]{2,1,0:T(8,128)(2,1)S(1)}, bf16[1,288,384]{2,1,0:T(8,128)(2,1)S(1)}, u32[]{:S(2)}, u32[]{:S(2)}) collective-permute-start(bf16[1,288,384]{2,1,0:T(8,128)(2,1)S(1)} %slice.100), channel_id=1, source_target_pairs={{4,0},{8,4},{12,8},{16,12},{20,16},{24,20},{28,24},{5,1},{9,5},{13... | collective-permute-start | bytes 663560 | tf_op jit(solution)/shard_map/ppermute | solution.py:13
  471.6 52.6 %copy-start.3 = (bf16[288,1536]{1,0:T(8,128)(2,1)S(1)}, bf16[288,1536]{1,0:T(8,128)(2,1)}, u32[]{:S(2)}) copy-start(bf16[288,1536]{1,0:T(8,128)(2,1)} %param.13) | copy-start | bytes 2654212
  471.6 54.3 %copy-start.6 = (bf16[288,1536]{1,0:T(8,128)(2,1)S(1)}, bf16[288,1536]{1,0:T(8,128)(2,1)}, u32[]{:S(2)}) copy-start(bf16[288,1536]{1,0:T(8,128)(2,1)} %copy-done.5) | copy-start | bytes 2654212
  524.3 1.7 copy-start.7
  524.3 1.7 copy-start.22
Sparse Core Ops, SparseCore 0:
  10.2 206.0 all-gather.1
  471.8 52.4 all-reduce.3
where the time goes:
time: 546 us; the launch traced here: 544 us
  waiting for transfers between devices  201 us (37%)
  matrix products  111 us (20%)
  starting transfers between devices  97.2 us (18%)
  local copies, waits for them, and re-layouts  59.4 us (11%)
  blocking collectives  36.7 us (7%)
  other arithmetic  23.5 us (4%)
  between operations  14.6 us (3%)
    ppermute x12, waiting for transfers between devices, shifted(): return lax.ppermute(array, axis, pairs)  122 us
    ppermute x12, starting transfers between devices, shifted(): return lax.ppermute(array, axis, pairs)  97.2 us
    dot_general x23, matrix products, times_rows(): lax.dot_general(left, right, (((1,), (1,)), ((), ())), preferred_element_...  54.5 us
    psum x1, waiting for transfers between devices, local(): summed = lax.psum(projected.astype(jnp.bfloat16), 'mp').astype(jnp.float32)  52.6 us
    psum x1, blocking collectives, local(): lax.psum(d_partial, 'mp').astype(jnp.bfloat16)  36.7 us
    all_gather x1, waiting for transfers between devices, local(): full_shorten = lax.all_gather(w_shorten, 'seq', axis=0, tiled=True)  26 us
    dot_general x12, matrix products, times_cols(): lax.dot_general(left, right, (((0,), (0,)), ((), ())), preferred_element_...  22 us
    unnamed x59, local copies, waits for them, and re-layouts  12.3 us
  transfers between devices with their start and end apart: 14, of which 11 were waited for; matrix products, arithmetic and copies ran while one was open for 17% of the time, Pallas kernels for 0%

commit v1 on v0

--- a/solution.py
+++ b/solution.py
@@ -1,10 +1,15 @@
+import functools
+
 import jax
 import jax.numpy as jnp
 from jax import lax
+from jax.experimental import pallas as pl
+from jax.experimental.pallas import tpu as pltpu
 from jax.sharding import PartitionSpec as P
 
 HEAD = 64
 WIN = 4096
+LANES = 2 * HEAD
 
 
 def shifted(array, axis, by):
@@ -42,7 +47,287 @@
     )
 
 
-def local(tokens, norm_gain, w_query, w_key, w_value, w_out, w_shorten, first_key, d_faces):
+def exchange_kernel(plan, heads, first_owner, *refs):
+    count = len(plan)
+    sources, targets = refs[:count], refs[count : 2 * count]
+    send_sems, recv_sems, own_sem = refs[2 * count :]
+    axes = sorted({axis for axis, _ in plan})
+    barrier = pltpu.get_barrier_semaphore()
+    greeted = 0
+    for axis in axes:
+        size = lax.axis_size(axis)
+        for step in range(1, size):
+            peer = lax.rem(lax.axis_index(axis) + step, size)
+            pl.semaphore_signal(
+                barrier, inc=1, device_id={axis: peer}, device_id_type=pl.DeviceIdType.MESH
+            )
+            greeted += 1
+    pl.semaphore_wait(barrier, greeted)
+
+    def owns(place):
+        return (place >= first_owner) & (place < first_owner + heads)
+
+    def when(condition, action):
+        if condition is None:
+            action()
+        else:
+            pl.when(condition)(action)
+
+    finals = []
+    for item, (axis, kind) in enumerate(plan):
+        source, target = sources[item], targets[item]
+        size = lax.axis_size(axis)
+        me = lax.axis_index(axis)
+        for step in list(range(1, size)) + [0]:
+            peer = lax.rem(me + step, size)
+            origin = lax.rem(me + size - step, size)
+            send_if = recv_if = None
+            if kind == "all":
+                piece, slot = source.at[peer], target.at[me]
+            elif kind == "same":
+                piece, slot = source, target.at[me]
+            elif kind == "to_heads":
+                piece = source.at[jnp.clip(peer - first_owner, 0, heads - 1)]
+                slot = target.at[me]
+                send_if, recv_if = owns(peer), owns(me)
+            else:
+                piece = source.at[peer]
+                slot = target.at[jnp.clip(me - first_owner, 0, heads - 1)]
+                send_if, recv_if = owns(me), owns(origin)
+            if step == 0:
+                copy = pltpu.make_async_copy(piece, slot, own_sem.at[item])
+                when(send_if, copy.start)
+                finals.append((send_if, copy.wait))
+            else:
+                copy = pltpu.make_async_remote_copy(
+                    src_ref=piece,
+                    dst_ref=slot,
+                    send_sem=send_sems.at[item, step],
+                    recv_sem=recv_sems.at[item, step],
+                    device_id={axis: peer},
+                    device_id_type=pl.DeviceIdType.MESH,
+                )
+                when(send_if, copy.start)
+                finals.append((send_if, copy.wait_send))
+                finals.append((recv_if, copy.wait_recv))
+    for condition, action in finals:
+        when(condition, action)
+
+
+def exchange(collective, items, heads=1):
+    plan, shapes = [], []
+    most = 1
+    for array, axis, kind in items:
+        size = lax.axis_size(axis)
+        most = max(most, size)
+        plan.append((axis, kind))
+        tail = array.shape if kind == "same" else array.shape[1:]
+        lead = heads if kind == "from_heads" else size
+        shapes.append(jax.ShapeDtypeStruct((lead, *tail), array.dtype))
+    first_owner = (lax.axis_size("seq") - heads) // 2
+    return pl.pallas_call(
+        functools.partial(exchange_kernel, tuple(plan), heads, first_owner),
+        out_shape=shapes,
+        in_specs=[pl.BlockSpec(memory_space=pl.ANY)] * len(plan),
+        out_specs=[pl.BlockSpec(memory_space=pl.ANY)] * len(plan),
+        scratch_shapes=[
+            pltpu.SemaphoreType.DMA((len(plan), most)),
+            pltpu.SemaphoreType.DMA((len(plan), most)),
+            pltpu.SemaphoreType.DMA((len(plan),)),
+        ],
+        compiler_params=pltpu.CompilerParams(collective_id=collective, has_side_effects=True),
+    )(*[array for array, _, _ in items])
+
+
+def attention_kernel(heads, tile, kv_ref, qd_ref, low_ref, dqa_ref, dkv_ref, probs, d_kv):
+    size = lax.axis_size("seq")
+    first_owner = (size - heads) // 2
+    me = lax.axis_index("seq")
+
+    @pl.when((me >= first_owner) & (me < first_owner + heads))
+    def _():
+        tiles = kv_ref.shape[0] // tile
+        d_kv[...] = jnp.zeros_like(d_kv)
+        low_half = lax.broadcasted_iota(jnp.int32, (tile, LANES), 1) < HEAD
+        row = lax.broadcasted_iota(jnp.int32, (tile, tile), 0)
+        col = lax.broadcasted_iota(jnp.int32, (tile, tile), 1)
+
+        def query_step(i, _):
+            here = pl.ds(pl.multiple_of(i * tile, tile), tile)
+            both = qd_ref[here, :]
+            query = jnp.where(low_half, both, jnp.zeros_like(both))
+            d_att = jnp.where(low_half, jnp.zeros_like(both), both)
+            lowest = jnp.maximum(low_ref[0:1, here], i * tile + col[0:1, :] - (WIN - 1))
+
+            def score_step(j, top):
+                there = pl.ds(pl.multiple_of(j * tile, tile), tile)
+                scores = times_rows(kv_ref[there, :], query)
+                pos_k = j * tile + row
+                allowed = (pos_k >= lowest) & (pos_k <= i * tile + col)
+                scores = jnp.where(allowed, scores, -1e30)
+                probs[j] = scores
+                return jnp.maximum(top, jnp.max(scores, axis=0, keepdims=True))
+
+            top = lax.fori_loop(
+                0, i + 1, score_step, jnp.full((1, tile), -1e30, jnp.float32)
+            )
+
+            def raise_step(j, total):
+                raised = jnp.exp(probs[j] - top)
+                probs[j] = raised
+                return total + jnp.sum(raised, axis=0, keepdims=True)
+
+            total = lax.fori_loop(0, i + 1, raise_step, jnp.zeros((1, tile), jnp.float32))
+            inverse = 1.0 / total
+
+            def forward_step(j, acc):
+                there = pl.ds(pl.multiple_of(j * tile, tile), tile)
+                short = (probs[j] * inverse).astype(jnp.bfloat16)
+                d_kv[there, :] += jnp.dot(short, d_att, preferred_element_type=jnp.float32)
+                return acc + times_cols(short, kv_ref[there, :])
+
+            zero = jnp.zeros((tile, LANES), jnp.float32)
+            attended = lax.fori_loop(0, i + 1, forward_step, zero).astype(jnp.bfloat16)
+            product = attended.astype(jnp.float32) * d_att.astype(jnp.float32)
+            delta = jnp.sum(product.T, axis=0, keepdims=True)
+
+            def backward_step(j, acc):
+                there = pl.ds(pl.multiple_of(j * tile, tile), tile)
+                d_probs = times_rows(kv_ref[there, :], d_att)
+                d_scores = (probs[j] * inverse * (d_probs - delta)).astype(jnp.bfloat16)
+                d_kv[there, :] += jnp.dot(d_scores, query, preferred_element_type=jnp.float32)
+                return acc + times_cols(d_scores, kv_ref[there, :])
+
+            d_query = lax.fori_loop(0, i + 1, backward_step, zero) * HEAD ** (-0.5)
+            dqa_ref[here, :] = jnp.where(low_half, d_query.astype(jnp.bfloat16), attended)
+            return 0
+
+        lax.fori_loop(0, tiles, query_step, 0)
+        dkv_ref[...] = d_kv[...].astype(jnp.bfloat16)
+
+
+def attention(heads, kv, qd, low):
+    total = kv.shape[0]
+    tile = next(size for size in (256, 128) if total % size == 0)
+    whole = pl.BlockSpec(memory_space=pltpu.VMEM)
+    return pl.pallas_call(
+        functools.partial(attention_kernel, heads, tile),
+        out_shape=[jax.ShapeDtypeStruct(kv.shape, jnp.bfloat16)] * 2,
+        in_specs=[whole] * 3,
+        out_specs=[whole] * 2,
+        scratch_shapes=[
+            pltpu.VMEM((total // tile, tile, tile), jnp.float32),
+            pltpu.VMEM((total, LANES), jnp.float32),
+        ],
+        compiler_params=pltpu.CompilerParams(vmem_limit_bytes=32 * 1024 * 1024),
+    )(kv, qd, low)
+
+
+def by_heads(left, right):
+    rows = left.shape[0]
+    pair = [part.reshape(rows, -1, HEAD) for part in (left, right)]
+    return jnp.concatenate(pair, axis=2).transpose(1, 0, 2)
+
+
+def from_heads(pair):
+    rows = pair.shape[1]
+    flat = pair.transpose(1, 0, 2)
+    return flat[:, :, :HEAD].reshape(rows, -1), flat[:, :, HEAD:].reshape(rows, -1)
+
+
+def by_head_owner(
+    tokens, norm_gain, w_query, w_key, w_value, w_out, w_shorten, first_key, d_faces
+):
+    tok_rows, model_width = tokens.shape
+    face_rows = tok_rows // 9
+    heads = w_query.shape[1] // HEAD
+    seq_count, mp_count = lax.axis_size("seq"), lax.axis_size("mp")
+    chunk = w_shorten.shape[0] // mp_count
+    padded = -(-chunk // 128) * 128
+    tok_total = tok_rows * seq_count
+    faces_total = face_rows * seq_count
+
+    bounds = jnp.broadcast_to(jnp.pad(first_key, (0, -face_rows % 128))[None], (8, -(-face_rows // 128) * 128))
+    all_d_faces, all_bounds = exchange(
+        1, [(d_faces, "seq", "same"), (bounds, "seq", "same")]
+    )
+    low = jnp.repeat(all_bounds[:, 0, :face_rows].reshape(faces_total), 9)[None]
+
+    shorten = jnp.pad(
+        w_shorten.reshape(mp_count, chunk, -1), ((0, 0), (0, padded - chunk), (0, 0))
+    )
+    d_partial = jnp.einsum(
+        "fc,mkc->mfk",
+        all_d_faces.reshape(faces_total, -1),
+        shorten,
+        preferred_element_type=jnp.float32,
+    ).astype(jnp.bfloat16)
+
+    x_float = tokens.astype(jnp.float32)
+    scale_r = lax.rsqrt(jnp.mean(x_float * x_float, axis=-1, keepdims=True) + 1e-05)
+    normed = (x_float * scale_r * norm_gain).astype(jnp.bfloat16)
+    query = jnp.dot(normed, w_query, preferred_element_type=jnp.float32).astype(jnp.bfloat16)
+    key = jnp.dot(normed, w_key, preferred_element_type=jnp.float32).astype(jnp.bfloat16)
+    value = jnp.dot(normed, w_value, preferred_element_type=jnp.float32).astype(jnp.bfloat16)
+
+    d_pieces, kv = exchange(
+        2, [(d_partial, "mp", "all"), (by_heads(key, value), "seq", "to_heads")], heads
+    )
+    d_chunk = jnp.sum(d_pieces.astype(jnp.float32), axis=0).astype(jnp.bfloat16)
+    (d_chunk,) = exchange(
+        3, [(d_chunk.reshape(seq_count, face_rows, padded), "seq", "all")]
+    )
+    (d_whole,) = exchange(4, [(d_chunk, "mp", "same")])
+    d_mixed = (
+        d_whole[..., :chunk].transpose(2, 1, 0, 3).reshape(tok_rows, model_width)
+    )
+    d_attended = times_rows(d_mixed, w_out).astype(jnp.bfloat16)
+    (qd,) = exchange(
+        5,
+        [(by_heads(query * jnp.bfloat16(HEAD ** (-0.5)), d_attended), "seq", "to_heads")],
+        heads,
+    )
+    dqa, dkv = attention(
+        heads, kv.reshape(tok_total, LANES), qd.reshape(tok_total, LANES), low
+    )
+    block = (seq_count, tok_rows, LANES)
+    dqa, dkv = exchange(
+        6,
+        [(dqa.reshape(block), "seq", "from_heads"), (dkv.reshape(block), "seq", "from_heads")],
+        heads,
+    )
+    d_query, attended = from_heads(dqa)
+    d_key, d_value = from_heads(dkv)
+    projected = jnp.dot(attended, w_out, preferred_element_type=jnp.float32).astype(jnp.bfloat16)
+    projected = projected.reshape(mp_count, tok_rows // mp_count, model_width)
+    part_normed = times_rows(d_query, w_query)
+    part_normed = part_normed + times_rows(d_key, w_key)
+    part_normed = part_normed + times_rows(d_value, w_value)
+    part_normed = part_normed.astype(jnp.bfloat16).reshape(projected.shape)
+    projected, part_normed = exchange(
+        7, [(projected, "mp", "all"), (part_normed, "mp", "all")]
+    )
+    projected = jnp.sum(projected.astype(jnp.float32), axis=0).astype(jnp.bfloat16)
+    part_normed = jnp.sum(part_normed.astype(jnp.float32), axis=0).astype(jnp.bfloat16)
+    summed, d_normed = exchange(
+        8, [(projected, "mp", "same"), (part_normed, "mp", "same")]
+    )
+    d_normed = d_normed.reshape(tok_rows, model_width).astype(jnp.float32)
+    summed = summed.reshape(tok_rows, model_width).astype(jnp.float32)
+    mixed = (x_float + summed).astype(jnp.bfloat16)
+    mixed = mixed.reshape(face_rows, seq_count, -1).transpose(1, 0, 2)
+    (mixed,) = exchange(9, [(mixed, "seq", "all")])
+    partial = jnp.dot(
+        mixed.reshape(faces_total, -1), w_shorten, preferred_element_type=jnp.float32
+    )
+    partial = partial.astype(jnp.bfloat16).reshape(seq_count, face_rows, -1)
+    (partial,) = exchange(10, [(partial, "seq", "all")])
+    faces = jnp.sum(partial.astype(jnp.float32), axis=0).astype(jnp.bfloat16)
+    d_tokens = finish(d_normed, x_float, scale_r, d_mixed, norm_gain).astype(jnp.bfloat16)
+    return (faces, d_tokens)
+
+
+def by_window(tokens, norm_gain, w_query, w_key, w_value, w_out, w_shorten, first_key, d_faces):
     tok_rows = tokens.shape[0]
     model_width = tokens.shape[1]
     face_rows = tok_rows // 9
@@ -156,6 +441,14 @@
     return (faces, d_tokens)
 
 
+def local(*arrays):
+    heads = arrays[2].shape[1] // HEAD
+    seq_count = lax.axis_size("seq")
+    if heads <= seq_count < 2 * heads:
+        return by_head_owner(*arrays)
+    return by_window(*arrays)
+
+
 def solution(mesh):
     in_specs = (
         P("seq", None),

time: 546 us -> 277 us (0.51)
  Pallas kernels: 0 us -> 215 us
  waiting for transfers between devices: 201 us -> 0 us
  starting transfers between devices: 97.2 us -> 0 us
  matrix products: 111 us -> 24.7 us
  local copies, waits for them, and re-layouts: 59.4 us -> 20.2 us
  blocking collectives: 36.7 us -> 0 us
  between operations: 14.6 us -> 0.95 us
  other arithmetic: 23.5 us -> 15.2 us
    pallas_call x0 -> x11, Pallas kernels: none -> 215 us  [the longest x10 215 us: exchange(): pl.pallas_call(functools.partial(exchange_kernel, tuple(plan), heads, fir...]
    ppermute x12 -> x0, waiting for transfers between devices: 122 us -> none  [shifted(): return lax.ppermute(array, axis, pairs)]
    ppermute x12 -> x0, starting transfers between devices: 97.2 us -> none  [shifted(): return lax.ppermute(array, axis, pairs)]
    psum x1 -> x0, waiting for transfers between devices: 52.6 us -> none  [local(): summed = lax.psum(projected.astype(jnp.bfloat16), 'mp').astype(jnp.float32)]
    dot_general x23 -> x4, matrix products: 54.5 us -> 11.4 us  [times_rows(): lax.dot_general(left, right, (((1,), (1,)), ((), ())), preferred_element_...]
    dot_general x29 -> x6, matrix products: 56.2 us -> 13.3 us  [the longest x1 3.03 us: by_head_owner(): jnp.einsum('fc,mkc->mfk', all_d_faces.reshape(faces_total, -1), shorten,...]
    psum x1 -> x0, blocking collectives: 36.7 us -> none  [local(): lax.psum(d_partial, 'mp').astype(jnp.bfloat16)]
    all_gather x1 -> x0, waiting for transfers between devices: 26 us -> none  [local(): full_shorten = lax.all_gather(w_shorten, 'seq', axis=0, tiled=True)]
  transfers between devices with their start and end apart: 14 -> 0, of which waited for: 11 -> 0; matrix products, arithmetic and copies ran while one was open for 17% -> 0% of each run, Pallas kernels for 0% -> 0%
where the time goes in v1:
time: 277 us; the launch traced here: 276 us
  Pallas kernels  215 us (78%)
  matrix products  24.7 us (9%)
  local copies, waits for them, and re-layouts  20.2 us (7%)
  other arithmetic  15.2 us (5%)
    pallas_call x10, Pallas kernels, exchange(): pl.pallas_call(functools.partial(exchange_kernel, tuple(plan), heads, fir...  215 us
    dot_general x4, matrix products, times_rows(): lax.dot_general(left, right, (((1,), (1,)), ((), ())), preferred_element_...  11.4 us

profile of v1, /device:TPU:0, one launch (start us, length us, event | category | flops | bytes accessed | tf_op | source)
XLA Modules:
  0.0 276.3 jit_solution(14157818889200244731)
XLA Ops:
  0.6 1.5 fusion.4
  2.2 2.3 convolution_convert_fusion.4
  4.7 0.3 copy.15
  5.0 1.9 convolution_convert_fusion.3
  7.2 0.3 copy.16
  7.5 1.0 maximum_bitcast_fusion.refs_1_
  8.5 0.6 broadcast_in_dim.4.refs_1_
  9.1 12.4 %shard_map.104 = (bf16[8,32,384]{2,1,0:T(8,128)(2,1)}, s32[8,8,128]{2,1,0:T(8,128)}) custom-call(bf16[32,384]{1,0:T(8,128)(2,1)} %refs_0_.1, s32[8,128]{1,0:T(8,128)} %broadcast_in_dim.4.refs_1_), custom_call_target="tpu_custom_call" | custom-call | tf_op jit(solution)/shard_map/pallas_call | solution.py:128
  21.5 3.0 %fusion.15.refs_0_ = bf16[4,256,512]{2,1,0:T(8,128)(2,1)} fusion(bf16[256,384,1]{1,0,2:T(8,128)(2,1)} %bitcast.77, bf16[4,432,384]{2,1,0:T(8,128)(2,1)} %bitcast.66), kind=kOutput, calls=%fused_computation.23 | convolution fusion | flops 403177472 | bytes 2572288 | tf_op jit(solution)/shard_map/fc,mkc->mfk/dot_general | solution.py:259
  24.5 13.9 %shard_map.105 = (bf16[4,256,512]{2,1,0:T(8,128)(2,1)}, bf16[8,288,128]{2,1,0:T(8,128)(2,1)}) custom-call(bf16[4,256,512]{2,1,0:T(8,128)(2,1)} %fusion.15.refs_0_, bf16[6,288,128]{2,1,0:T(8,128)(2,1)} %maximum_bitcast_fusion.refs_1_), custom_call_target="tpu_custom_call" | custom-call | tf_op jit(solution)/shard_map/pallas_call | solution.py:128
  38.5 2.2 reduce_sum.67
  40.6 9.1 %shard_map.106.refs_0_ = bf16[8,32,512]{2,1,0:T(8,128)(2,1)} custom-call(bf16[8,32,512]{2,1,0:T(8,128)(2,1)} %bitcast.75), custom_call_target="tpu_custom_call" | custom-call | tf_op jit(solution)/shard_map/pallas_call | solution.py:128
  49.8 13.4 %shard_map.107 = bf16[4,8,32,512]{3,2,1,0:T(8,128)(2,1)} custom-call(bf16[8,32,512]{2,1,0:T(8,128)(2,1)} %shard_map.106.refs_0_), custom_call_target="tpu_custom_call" | custom-call | tf_op jit(solution)/shard_map/pallas_call | solution.py:128
  63.2 1.3 slice_bitcast_fusion
  64.5 0.8 copy.18
  65.3 3.0 %reshape.100 = bf16[288,1536]{1,0:T(8,128)(2,1)} reshape(bf16[32,8,4,432]{3,2,1,0:T(4,128)(2,1)S(1)} %copy.18) | data formatting | bytes 1769472 | tf_op jit(solution)/shard_map/reshape | solution.py:282
  68.3 2.2 convolution_convert_fusion.1
  70.7 0.3 copy.21
  71.0 0.7 fusion.18
  71.7 0.9 copy.17
  72.6 1.3 copy.20
  73.8 1.0 maximum_bitcast_fusion.1.refs_0_
  74.8 13.6 %shard_map.108 = bf16[8,288,128]{2,1,0:T(8,128)(2,1)} custom-call(bf16[6,288,128]{2,1,0:T(8,128)(2,1)} %maximum_bitcast_fusion.1.refs_0_), custom_call_target="tpu_custom_call" | custom-call | tf_op jit(solution)/shard_map/pallas_call | solution.py:128
  88.5 0.8 slice_reduce_fusion
  89.7 1.1 copy-done.1
  90.7 0.8 copy-done.2
  91.6 0.8 copy-done.3
  92.4 72.6 %shard_map.110 = (bf16[6,288,128]{2,1,0:T(8,128)(2,1)}, bf16[6,288,128]{2,1,0:T(8,128)(2,1)}) custom-call(bf16[8,288,128]{2,1,0:T(8,128)(2,1)} %bitcast.57, bf16[8,288,128]{2,1,0:T(8,128)(2,1)} %bitcast.58), custom_call_target="tpu_custom_call" | custom-call | tf_op jit(solution)/shard_map/pallas_call | solution.py:128
  165.0 1.3 fusion.24
  166.3 0.3 copy.23
  166.6 1.9 fusion.25
  168.7 0.9 copy.24
  169.7 3.9 %convolution_add_fusion.1 = f32[288,1536]{1,0:T(8,128)} fusion(f32[288,1536]{1,0:T(8,128)} %fusion.25, bf16[288,384]{0,1:T(8,128)(2,1)} %bitcast.67, bf16[1536,384]{1,0:T(8,128)(2,1)} %param.12), kind=kOutput, calls=%fused_computation.6 | convolution fusion | flops 340180992 | bytes 4939776 | tf_op jit(solution)/shard_map/dot_general | solution.py:30
  173.8 3.4 %fusion = bf16[288,1536]{1,0:T(8,128)(2,1)} fusion(f32[288,1536]{1,0:T(8,128)} %convolution_add_fusion.1, bf16[288,384]{0,1:T(8,128)(2,1)S(1)} %bitcast.68, bf16[1536,384]{1,0:T(8,128)(2,1)} %param.13), kind=kOutput, calls=%fused_computation.8 | convolution fusion | flops 340623360 | bytes 4055040 | tf_op jit(solution)/shard_map/dot_general | solution.py:30
  177.2 0.3 copy.22
  177.5 2.8 %convolution_convert_fusion = bf16[288,1536]{1,0:T(8,128)(2,1)} fusion(bf16[288,384]{0,1:T(8,128)(2,1)S(1)} %bitcast.70, bf16[384,1536]{1,0:T(8,128)(2,1)} %param.14), kind=kOutput, calls=%fused_computation.7 | convolution fusion | flops 340180992 | bytes 2285568 | tf_op jit(solution)/shard_map/dot_general | solution.py:301
  180.3 22.0 %shard_map.111 = (bf16[4,72,1536]{2,1,0:T(8,128)(2,1)}, bf16[4,72,1536]{2,1,0:T(8,128)(2,1)}) custom-call(bf16[4,72,1536]{2,1,0:T(8,128)(2,1)} %bitcast.61, bf16[4,72,1536]{2,1,0:T(8,128)(2,1)} %bitcast.62), custom_call_target="tpu_custom_call" | custom-call | tf_op jit(solution)/shard_map/pallas_call | solution.py:128
  202.4 2.1 reduce_sum.68.refs_0_
  204.4 2.1 reduce_sum.69.refs_1_
  206.5 21.9 %shard_map.112 = (bf16[4,72,1536]{2,1,0:T(8,128)(2,1)}, bf16[4,72,1536]{2,1,0:T(8,128)(2,1)}) custom-call(bf16[72,1536]{1,0:T(8,128)(2,1)} %reduce_sum.68.refs_0_, bf16[72,1536]{1,0:T(8,128)(2,1)} %reduce_sum.69.refs_1_), custom_call_target="tpu_custom_call" | custom-call | tf_op jit(solution)/shard_map/pallas_call | solution.py:128
  228.5 1.7 fusion.9
  230.2 2.0 fusion.3
  232.2 2.6 reshape.111
  234.8 1.1 copy.29
  235.9 23.0 %shard_map.113 = bf16[8,32,1728]{2,1,0:T(8,128)(2,1)} custom-call(bf16[8,32,1728]{2,1,0:T(8,128)(2,1)} %bitcast.60), custom_call_target="tpu_custom_call" | custom-call | tf_op jit(solution)/shard_map/pallas_call | solution.py:128
  258.9 2.5 convolution_convert_fusion.5
  261.4 13.3 %shard_map.114 = bf16[8,32,384]{2,1,0:T(8,128)(2,1)} custom-call(bf16[8,32,384]{2,1,0:T(8,128)(2,1)} %bitcast.78), custom_call_target="tpu_custom_call" | custom-call | tf_op jit(solution)/shard_map/pallas_call | solution.py:128
  274.7 1.6 reduce_sum.70
  (35 shorter events, 1.6 us)
Async XLA Ops:
  0.6 70.3 %copy-start = (bf16[1536,384]{1,0:T(8,128)(2,1)S(1)}, bf16[1536,384]{1,0:T(8,128)(2,1)}, u32[]{:S(2)}) copy-start(bf16[1536,384]{1,0:T(8,128)(2,1)} %param.11) | copy-start | bytes 3538948
  2.2 2.8 %copy-start.5 = (bf16[288,1536]{1,0:T(8,128)(2,1)S(1)}, bf16[288,1536]{1,0:T(8,128)(2,1)}, u32[]{:S(2)}) copy-start(bf16[288,1536]{1,0:T(8,128)(2,1)} %param.9) | copy-start | bytes 2654212
  2.2 2.8 %copy-start.11 = (f32[1536]{0:T(1024)S(1)}, f32[1536]{0:T(1024)}, u32[]{:S(2)}) copy-start(f32[1536]{0:T(1024)} %param.10) | copy-start | bytes 18436
  7.0 1.5 copy-start.12
  72.5 17.1 %copy-start.4 = (bf16[8,288,128]{2,1,0:T(8,128)(2,1)S(1)}, bf16[8,288,128]{2,1,0:T(8,128)(2,1)}, u32[]{:S(2)}) copy-start(bf16[8,288,128]{2,1,0:T(8,128)(2,1)} %get-tuple-element.15) | copy-start | bytes 1769476
  89.7 1.1 copy-start.1
  90.7 0.8 copy-start.2
  91.6 0.8 copy-start.3
  166.6 1.9 copy-start.8
  204.4 25.7 %copy-start.6 = (bf16[288,1536]{1,0:T(8,128)(2,1)S(1)}, bf16[288,1536]{1,0:T(8,128)(2,1)}, u32[]{:S(2)}) copy-start(bf16[288,1536]{1,0:T(8,128)(2,1)} %reshape.100) | copy-start | bytes 2654212
  228.4 1.7 copy-start.7
  228.4 1.7 copy-start.10
  235.9 23.0 %copy-start.9 = (bf16[1728,384]{1,0:T(8,128)(2,1)S(1)}, bf16[1728,384]{1,0:T(8,128)(2,1)}, u32[]{:S(2)}) copy-start(bf16[1728,384]{1,0:T(8,128)(2,1)} %param.15) | copy-start | bytes 3981316

commit v2 on v0

--- a/solution.py
+++ b/solution.py
@@ -1,10 +1,15 @@
+import functools
+
 import jax
 import jax.numpy as jnp
 from jax import lax
+from jax.experimental import pallas as pl
+from jax.experimental.pallas import tpu as pltpu
 from jax.sharding import PartitionSpec as P
 
 HEAD = 64
 WIN = 4096
+LANES = 2 * HEAD
 
 
 def shifted(array, axis, by):
@@ -42,7 +47,457 @@
     )
 
 
-def local(tokens, norm_gain, w_query, w_key, w_value, w_out, w_shorten, first_key, d_faces):
+def exchange_kernel(plan, heads, first_owner, *refs):
+    count = len(plan)
+    sources, targets = refs[:count], refs[count : 2 * count]
+    send_sems, recv_sems, own_sem = refs[2 * count : 2 * count + 3]
+    spares = refs[2 * count + 3 :]
+    barrier = pltpu.get_barrier_semaphore()
+    greeted = 0
+    for axis in sorted({axis for axis, _ in plan}):
+        size = lax.axis_size(axis)
+        for step in range(1, size):
+            peer = lax.rem(lax.axis_index(axis) + step, size)
+            pl.semaphore_signal(
+                barrier, inc=1, device_id={axis: peer}, device_id_type=pl.DeviceIdType.MESH
+            )
+            greeted += 1
+    pl.semaphore_wait(barrier, greeted)
+
+    def owns(place):
+        return (place >= first_owner) & (place < first_owner + heads)
+
+    def when(condition, action):
+        if condition is None:
+            action()
+        else:
+            pl.when(condition)(action)
+
+    def remote(item, step, piece, slot, axis, peer):
+        return pltpu.make_async_remote_copy(
+            src_ref=piece,
+            dst_ref=slot,
+            send_sem=send_sems.at[item, step],
+            recv_sem=recv_sems.at[item, step],
+            device_id={axis: peer},
+            device_id_type=pl.DeviceIdType.MESH,
+        )
+
+    finals = []
+    paired = []
+    for item, (axis, kind) in sorted(enumerate(plan), key=lambda pair: pair[1][1] not in PAIRED):
+        source, target = sources[item], targets[item]
+        size = lax.axis_size(axis)
+        me = lax.axis_index(axis)
+        if kind in PAIRED:
+            near = me + 1 - 2 * lax.rem(me, 2)
+            far = lax.rem(me + 2, 4)
+            far_near = lax.rem(near + 2, 4)
+            link = functools.partial(remote, item)
+            if kind == "gather":
+                own = pltpu.make_async_copy(source, target.at[me], own_sem.at[item])
+                own.start()
+                first = [
+                    link(0, source, target.at[me], axis, far),
+                    link(1, source, target.at[me], axis, near),
+                ]
+                second = link(2, target.at[far], target.at[far], axis, near)
+            else:
+                came, joined, crossed = spares[:3]
+                spares = spares[3:]
+                first = [
+                    link(0, source.at[far_near], came.at[0], axis, near),
+                    link(1, source.at[near], came.at[1], axis, near),
+                ]
+                second = link(2, joined, crossed, axis, far)
+                own = None
+            for copy in first:
+                copy.start()
+            paired.append((item, kind, me, far, first, second, own))
+            if kind == "reduce":
+                paired[-1] += (came, joined, crossed)
+            continue
+        for step in list(range(1, size)) + [0]:
+            peer = lax.rem(me + step, size)
+            origin = lax.rem(me + size - step, size)
+            send_if = recv_if = None
+            if kind == "all":
+                piece, slot = source.at[peer], target.at[me]
+            elif kind == "same":
+                piece, slot = source, target.at[me]
+            elif kind == "to_heads":
+                piece = source.at[jnp.clip(peer - first_owner, 0, heads - 1)]
+                slot = target.at[me]
+                send_if, recv_if = owns(peer), owns(me)
+            else:
+                piece = source.at[peer]
+                slot = target.at[jnp.clip(me - first_owner, 0, heads - 1)]
+                send_if, recv_if = owns(me), owns(origin)
+            if step == 0:
+                copy = pltpu.make_async_copy(piece, slot, own_sem.at[item])
+                when(send_if, copy.start)
+                finals.append((send_if, copy.wait))
+            else:
+                copy = remote(item, step, piece, slot, axis, peer)
+                when(send_if, copy.start)
+                finals.append((send_if, copy.wait_send))
+                finals.append((recv_if, copy.wait_recv))
+
+    def added(left, right):
+        return (left.astype(jnp.float32) + right.astype(jnp.float32)).astype(jnp.bfloat16)
+
+    for item, kind, me, far, first, second, own, *held in paired:
+        if kind == "gather":
+            first[0].wait_recv()
+            second.start()
+        else:
+            came, joined, crossed = held
+            first[0].wait_recv()
+            joined[...] = added(sources[item][far], came[0])
+            second.start()
+    for item, kind, me, far, first, second, own, *held in paired:
+        if kind == "gather":
+            first[0].wait_send()
+            first[1].wait()
+            second.wait()
+            own.wait()
+        else:
+            came, joined, crossed = held
+            first[1].wait_recv()
+            mine = sources[item][me].astype(jnp.float32) + came[1].astype(jnp.float32)
+            second.wait_recv()
+            targets[item][...] = (mine + crossed[...].astype(jnp.float32)).astype(jnp.bfloat16)
+            first[0].wait_send()
+            first[1].wait_send()
+            second.wait_send()
+    for condition, action in finals:
+        when(condition, action)
+
+
+PAIRED = ("gather", "reduce")
+
+
+def exchange(collective, items, heads=1):
+    plan, shapes, spares, in_specs, out_specs = [], [], [], [], []
+    most = 3
+    for array, axis, kind in items:
+        size = lax.axis_size(axis)
+        most = max(most, size)
+        plan.append((axis, kind))
+        tail = array.shape if kind in ("same", "gather") else array.shape[1:]
+        lead = heads if kind == "from_heads" else size
+        space = pl.ANY
+        if kind == "reduce":
+            shapes.append(jax.ShapeDtypeStruct(tail, array.dtype))
+            spares.append(pltpu.VMEM((2, *tail), array.dtype))
+            spares += [pltpu.VMEM(tail, array.dtype)] * 2
+            space = pltpu.VMEM
+        else:
+            shapes.append(jax.ShapeDtypeStruct((lead, *tail), array.dtype))
+        in_specs.append(pl.BlockSpec(memory_space=space))
+        out_specs.append(pl.BlockSpec(memory_space=space))
+    first_owner = (lax.axis_size("seq") - heads) // 2
+    return pl.pallas_call(
+        functools.partial(exchange_kernel, tuple(plan), heads, first_owner),
+        out_shape=shapes,
+        in_specs=in_specs,
+        out_specs=out_specs,
+        scratch_shapes=[
+            pltpu.SemaphoreType.DMA((len(plan), most)),
+            pltpu.SemaphoreType.DMA((len(plan), most)),
+            pltpu.SemaphoreType.DMA((len(plan),)),
+            *spares,
+        ],
+        compiler_params=pltpu.CompilerParams(
+            collective_id=collective, has_side_effects=True, vmem_limit_bytes=24 * 1024 * 1024
+        ),
+    )(*[array for array, _, _ in items])
+
+
+def when_owner(heads, action):
+    first_owner = (lax.axis_size("seq") - heads) // 2
+    me = lax.axis_index("seq")
+    pl.when((me >= first_owner) & (me < first_owner + heads))(action)
+
+
+def rolled(array):
+    return pltpu.roll(array.astype(jnp.float32), HEAD, 1)
+
+
+def unpack(packed_ref, flat_ref, upper):
+    blocks, half, _ = packed_ref.shape
+    low_half = lax.broadcasted_iota(jnp.int32, (half, LANES), 1) < HEAD
+    for block in range(blocks):
+        packed = packed_ref[block]
+        other = rolled(packed).astype(packed.dtype)
+        parts = (other, packed) if upper else (packed, other)
+        zero = jnp.zeros_like(packed)
+        for place, part in enumerate(parts):
+            part = jnp.where(low_half, zero, part) if upper else jnp.where(low_half, part, zero)
+            flat_ref[pl.ds((2 * block + place) * half, half), :] = part
+
+
+def pack(flat_ref, packed_ref, upper):
+    blocks, half, _ = packed_ref.shape
+    low_half = lax.broadcasted_iota(jnp.int32, (half, LANES), 1) < HEAD
+    for block in range(blocks):
+        top = flat_ref[pl.ds(2 * block * half, half), :]
+        bottom = flat_ref[pl.ds((2 * block + 1) * half, half), :]
+        if upper:
+            top = rolled(top).astype(top.dtype)
+        else:
+            bottom = rolled(bottom).astype(top.dtype)
+        packed_ref[block] = jnp.where(low_half, top, bottom)
+
+
+def masked_scores(kv, query, lowest, key_start, query_start):
+    scores = times_rows(kv, query)
+    pos_k = key_start + lax.broadcasted_iota(jnp.int32, scores.shape, 0)
+    pos_q = query_start + lax.broadcasted_iota(jnp.int32, (1, scores.shape[1]), 1)
+    allowed = (pos_k >= jnp.maximum(lowest, pos_q - (WIN - 1))) & (pos_k <= pos_q)
+    return jnp.where(allowed, scores, -1e30)
+
+
+def forward_kernel(
+    heads, tile, span, kv_ref, packed_ref, low_ref, out_ref, query_ref, att_ref, top_ref, inv_ref
+):
+    def run():
+        unpack(packed_ref, query_ref, False)
+        high_half = lax.broadcasted_iota(jnp.int32, (tile, LANES), 1) >= HEAD
+
+        def query_step(i, _):
+            here = pl.ds(pl.multiple_of(i * tile, tile), tile)
+            query = query_ref[here, :]
+            lowest = low_ref[0:1, here]
+
+            def key_step(j, carry):
+                top, total, acc = carry
+                kv = kv_ref[pl.ds(pl.multiple_of(j * span, span), span), :]
+                scores = masked_scores(kv, query, lowest, j * span, i * tile)
+                new_top = jnp.maximum(top, jnp.max(scores, axis=0, keepdims=True))
+                raised = jnp.exp(scores - new_top)
+                shrink = jnp.exp(top - new_top)
+                total = total * shrink + jnp.sum(raised, axis=0, keepdims=True)
+                acc = acc * shrink + times_cols(kv, raised.astype(jnp.bfloat16))
+                return new_top, total, acc
+
+            start = (
+                jnp.full((1, tile), -1e30, jnp.float32),
+                jnp.zeros((1, tile), jnp.float32),
+                jnp.zeros((LANES, tile), jnp.float32),
+            )
+            top, total, acc = lax.fori_loop(0, (i * tile + tile - 1) // span + 1, key_step, start)
+            inverse = 1.0 / total
+            top_ref[0:1, here] = top
+            inv_ref[0:1, here] = inverse
+            attended = (acc * inverse).T.astype(jnp.bfloat16)
+            att_ref[here, :] = jnp.where(high_half, attended, jnp.zeros_like(attended))
+            return 0
+
+        lax.fori_loop(0, kv_ref.shape[0] // tile, query_step, 0)
+        pack(att_ref, out_ref, True)
+
+    when_owner(heads, run)
+
+
+def backward_kernel(
+    heads, tile, span, kv_ref, query_ref, packed_ref, low_ref, att_ref, top_ref, inv_ref,
+    dq_out, dkv_out, d_att_ref, dq_ref, d_kv,
+):
+    def run():
+        unpack(packed_ref, d_att_ref, True)
+        d_kv[...] = jnp.zeros_like(d_kv)
+
+        def query_step(i, _):
+            here = pl.ds(pl.multiple_of(i * tile, tile), tile)
+            query, d_att = query_ref[here, :], d_att_ref[here, :]
+            lowest, top, inverse = low_ref[0:1, here], top_ref[0:1, here], inv_ref[0:1, here]
+            product = att_ref[here, :].astype(jnp.float32) * d_att.astype(jnp.float32)
+            delta = jnp.sum(product.T, axis=0, keepdims=True)
+
+            def key_step(j, acc):
+                there = pl.ds(pl.multiple_of(j * span, span), span)
+                kv = kv_ref[there, :]
+                scores = masked_scores(kv, query, lowest, j * span, i * tile)
+                probs = jnp.exp(scores - top) * inverse
+                d_probs = times_rows(kv, d_att)
+                d_scores = (probs * (d_probs - delta)).astype(jnp.bfloat16)
+                d_kv[there, :] += jnp.dot(
+                    d_scores, query, preferred_element_type=jnp.float32
+                ) + jnp.dot(
+                    probs.astype(jnp.bfloat16), d_att, preferred_element_type=jnp.float32
+                )
+                return acc + times_cols(kv, d_scores)
+
+            zero = jnp.zeros((LANES, tile), jnp.float32)
+            acc = lax.fori_loop(0, (i * tile + tile - 1) // span + 1, key_step, zero)
+            dq_ref[here, :] = (acc * HEAD ** (-0.5)).T.astype(jnp.bfloat16)
+            return 0
+
+        lax.fori_loop(0, kv_ref.shape[0] // tile, query_step, 0)
+        dkv_out[...] = d_kv[...].astype(jnp.bfloat16)
+        pack(dq_ref, dq_out, False)
+
+    when_owner(heads, run)
+
+
+def tiling(total):
+    tile = next(size for size in (256, 128) if total % size == 0)
+    return tile, tile * (3 if total % (3 * tile) == 0 else 1)
+
+
+def plain_call(body, arrays, shapes, scratch=()):
+    whole = pl.BlockSpec(memory_space=pltpu.VMEM)
+    return pl.pallas_call(
+        body,
+        out_shape=[jax.ShapeDtypeStruct(*shape) for shape in shapes],
+        in_specs=[whole] * len(arrays),
+        out_specs=[whole] * len(shapes),
+        scratch_shapes=list(scratch),
+        compiler_params=pltpu.CompilerParams(vmem_limit_bytes=32 * 1024 * 1024),
+    )(*arrays)
+
+
+def by_heads(left, right):
+    rows = left.shape[0]
+    pair = [part.reshape(rows, -1, HEAD) for part in (left, right)]
+    return jnp.concatenate(pair, axis=2).transpose(1, 0, 2)
+
+
+def packed_heads(array):
+    half = array.shape[0] // 2
+    return by_heads(array[:half], array[half:])
+
+
+def from_heads(pair):
+    rows = pair.shape[1]
+    flat = pair.transpose(1, 0, 2)
+    return flat[:, :, :HEAD].reshape(rows, -1), flat[:, :, HEAD:].reshape(rows, -1)
+
+
+def unpacked_heads(pair):
+    return jnp.concatenate(from_heads(pair), axis=0)
+
+
+def by_head_owner(
+    tokens, norm_gain, w_query, w_key, w_value, w_out, w_shorten, first_key, d_faces
+):
+    tok_rows, model_width = tokens.shape
+    face_rows = tok_rows // 9
+    heads = w_query.shape[1] // HEAD
+    seq_count, mp_count = lax.axis_size("seq"), lax.axis_size("mp")
+    chunk = w_shorten.shape[0] // mp_count
+    padded = -(-chunk // 128) * 128
+    tok_total = tok_rows * seq_count
+    faces_total = face_rows * seq_count
+    bf16, f32 = jnp.bfloat16, jnp.float32
+
+    wide = -(-face_rows // 128) * 128
+    bounds = jnp.broadcast_to(jnp.pad(first_key, (0, wide - face_rows))[None], (8, wide))
+    all_d_faces, all_bounds = exchange(
+        1, [(d_faces, "seq", "same"), (bounds, "seq", "same")]
+    )
+    low = jnp.repeat(all_bounds[:, 0, :face_rows].reshape(faces_total), 9)[None]
+
+    shorten = jnp.pad(
+        w_shorten.reshape(mp_count, chunk, -1), ((0, 0), (0, padded - chunk), (0, 0))
+    )
+    d_partial = jnp.einsum(
+        "fc,mkc->mfk",
+        all_d_faces.reshape(faces_total, -1),
+        shorten,
+        preferred_element_type=f32,
+    ).astype(bf16)
+
+    x_float = tokens.astype(f32)
+    scale_r = lax.rsqrt(jnp.mean(x_float * x_float, axis=-1, keepdims=True) + 1e-05)
+    normed = (x_float * scale_r * norm_gain).astype(bf16)
+    query = jnp.dot(normed, w_query, preferred_element_type=f32).astype(bf16)
+    key = jnp.dot(normed, w_key, preferred_element_type=f32).astype(bf16)
+    value = jnp.dot(normed, w_value, preferred_element_type=f32).astype(bf16)
+
+    kv, packed_query, d_chunk = exchange(
+        2,
+        [
+            (by_heads(key, value), "seq", "to_heads"),
+            (packed_heads(query * bf16(HEAD ** (-0.5))), "seq", "to_heads"),
+            (d_partial, "mp", "reduce"),
+        ],
+        heads,
+    )
+    kv = kv.reshape(tok_total, LANES)
+    tile, span = tiling(tok_total)
+    flat = ((tok_total, LANES), bf16)
+    folded = ((seq_count, tok_rows // 2, LANES), bf16)
+    line = ((1, tok_total), f32)
+    att_packed, query_flat, att_flat, top, inverse = plain_call(
+        functools.partial(forward_kernel, heads, tile, span),
+        (kv, packed_query, low),
+        (folded, flat, flat, line, line),
+    )
+    att_packed, d_chunk = exchange(
+        3,
+        [
+            (att_packed, "seq", "from_heads"),
+            (d_chunk.reshape(seq_count, face_rows, padded), "seq", "all"),
+        ],
+        heads,
+    )
+    attended = unpacked_heads(att_packed)
+    projected = jnp.dot(attended, w_out, preferred_element_type=f32) + x_float / mp_count
+    projected = projected.astype(bf16).reshape(face_rows, seq_count, mp_count, chunk)
+    projected = jnp.pad(projected, ((0, 0), (0, 0), (0, 0), (0, padded - chunk)))
+    projected = projected.transpose(2, 1, 0, 3).reshape(mp_count, faces_total, padded)
+    d_whole, mixed = exchange(4, [(d_chunk, "mp", "gather"), (projected, "mp", "reduce")])
+    d_mixed = d_whole[..., :chunk].transpose(2, 1, 0, 3).reshape(tok_rows, model_width)
+    d_attended = times_rows(d_mixed, w_out).astype(bf16)
+    d_att_packed, mixed = exchange(
+        5,
+        [
+            (packed_heads(d_attended), "seq", "to_heads"),
+            (mixed.reshape(seq_count, face_rows, padded), "seq", "all"),
+        ],
+        heads,
+    )
+    d_query, d_kv = plain_call(
+        functools.partial(backward_kernel, heads, tile, span),
+        (kv, query_flat, d_att_packed, low, att_flat, top, inverse),
+        (folded, flat),
+        [pltpu.VMEM(*flat), pltpu.VMEM(*flat), pltpu.VMEM(flat[0], f32)],
+    )
+    d_query, d_kv, mixed = exchange(
+        6,
+        [
+            (d_query, "seq", "from_heads"),
+            (d_kv.reshape(seq_count, tok_rows, LANES), "seq", "from_heads"),
+            (mixed, "mp", "gather"),
+        ],
+        heads,
+    )
+    partial = jnp.einsum(
+        "mfk,mkc->fc",
+        mixed.reshape(mp_count, faces_total, padded),
+        shorten,
+        preferred_element_type=f32,
+    )
+    partial = partial.astype(bf16).reshape(seq_count, face_rows, -1)
+    d_query = unpacked_heads(d_query)
+    d_key, d_value = from_heads(d_kv)
+    part_normed = times_rows(d_query, w_query)
+    part_normed = part_normed + times_rows(d_key, w_key)
+    part_normed = part_normed + times_rows(d_value, w_value)
+    part_normed = part_normed.astype(bf16).reshape(mp_count, tok_rows // mp_count, model_width)
+    part_normed, partial = exchange(
+        7, [(part_normed, "mp", "reduce"), (partial, "seq", "all")]
+    )
+    (d_normed,) = exchange(8, [(part_normed, "mp", "gather")])
+    faces = jnp.sum(partial.astype(f32), axis=0).astype(bf16)
+    d_normed = d_normed.reshape(tok_rows, model_width).astype(f32)
+    d_tokens = finish(d_normed, x_float, scale_r, d_mixed, norm_gain).astype(bf16)
+    return (faces, d_tokens)
+
+
+def by_window(tokens, norm_gain, w_query, w_key, w_value, w_out, w_shorten, first_key, d_faces):
     tok_rows = tokens.shape[0]
     model_width = tokens.shape[1]
     face_rows = tok_rows // 9
@@ -156,6 +611,14 @@
     return (faces, d_tokens)
 
 
+def local(*arrays):
+    heads = arrays[2].shape[1] // HEAD
+    seq_count = lax.axis_size("seq")
+    if heads <= seq_count < 2 * heads and lax.axis_size("mp") == 4:
+        return by_head_owner(*arrays)
+    return by_window(*arrays)
+
+
 def solution(mesh):
     in_specs = (
         P("seq", None),

time: 546 us -> 198 us (0.36)
  waiting for transfers between devices: 201 us -> 0 us
  Pallas kernels: 0 us -> 146 us
  starting transfers between devices: 97.2 us -> 0 us
  matrix products: 111 us -> 17.4 us
  blocking collectives: 36.7 us -> 0 us
  local copies, waits for them, and re-layouts: 59.4 us -> 26.3 us
  other arithmetic: 23.5 us -> 6.63 us
  between operations: 14.6 us -> 1.04 us
    pallas_call x0 -> x10, Pallas kernels: none -> 146 us  [the longest x8 146 us: exchange(): pl.pallas_call(functools.partial(exchange_kernel, tuple(plan), heads, fir...]
    ppermute x12 -> x0, waiting for transfers between devices: 122 us -> none  [shifted(): return lax.ppermute(array, axis, pairs)]
    ppermute x12 -> x0, starting transfers between devices: 97.2 us -> none  [shifted(): return lax.ppermute(array, axis, pairs)]
    psum x1 -> x0, waiting for transfers between devices: 52.6 us -> none  [local(): summed = lax.psum(projected.astype(jnp.bfloat16), 'mp').astype(jnp.float32)]
    dot_general x23 -> x4, matrix products: 54.5 us -> 5.42 us  [times_rows(): lax.dot_general(left, right, (((1,), (1,)), ((), ())), preferred_element_...]
    dot_general x29 -> x6, matrix products: 56.2 us -> 12 us  [the longest x1 3.01 us: by_head_owner(): jnp.dot(attended, w_out, preferred_element_type=f32) + x_float / mp_count]
    psum x1 -> x0, blocking collectives: 36.7 us -> none  [local(): lax.psum(d_partial, 'mp').astype(jnp.bfloat16)]
    all_gather x1 -> x0, waiting for transfers between devices: 26 us -> none  [local(): full_shorten = lax.all_gather(w_shorten, 'seq', axis=0, tiled=True)]
  transfers between devices with their start and end apart: 14 -> 0, of which waited for: 11 -> 0; matrix products, arithmetic and copies ran while one was open for 17% -> 0% of each run, Pallas kernels for 0% -> 0%
where the time goes in v2:
time: 198 us; the launch traced here: 197 us
  Pallas kernels  146 us (74%)
  local copies, waits for them, and re-layouts  26.3 us (13%)
  matrix products  17.4 us (9%)
  other arithmetic  6.63 us (3%)
    pallas_call x8, Pallas kernels, exchange(): pl.pallas_call(functools.partial(exchange_kernel, tuple(plan), heads, fir...  146 us
    reshape x2, local copies, waits for them, and re-layouts, by_head_owner(): projected.astype(bf16).reshape(face_rows, seq_count, mp_count, chunk)  6.33 us
    dot_general x4, matrix products, times_rows(): lax.dot_general(left, right, (((1,), (1,)), ((), ())), preferred_element_...  5.42 us
    reshape x1, local copies, waits for them, and re-layouts, by_head_owner(): d_whole[..., :chunk].transpose(2, 1, 0, 3).reshape(tok_rows, model_width)  3.97 us

profile of v2, /device:TPU:0, one launch (start us, length us, event | category | flops | bytes accessed | tf_op | source)
XLA Modules:
  0.0 197.3 jit_solution(9756503185975641831)
XLA Ops:
  0.6 0.8 pad.13
  1.4 1.4 fusion.5
  2.9 2.3 %convolution_convert_fusion.2 = bf16[288,384]{1,0:T(8,128)(2,1)S(1)} fusion(bf16[1536,384]{1,0:T(8,128)(2,1)} %param.13, bf16[288,1536]{1,0:T(8,128)(2,1)} %param.9, f32[1536]{0:T(1024)} %param.10, f32[288]{0:T(512)S(1)} %get-tuple-element.59), kind=kOutput, calls=%fused_computation.29 | convolution fusion | flops 341618688 | bytes 2292864 | tf_op jit(solution)/shard_map/dot_general | solution.py:417
  5.2 0.2 copy.14
  5.4 0.3 copy.16
  5.7 2.0 fusion.26
  7.9 0.2 copy.19
  8.2 0.2 copy.20
  8.5 2.0 convolution_convert_fusion.3
  10.5 0.2 copy.13
  10.7 0.3 copy.15
  11.0 0.3 maximum_bitcast_fusion.refs_0_
  11.3 12.1 %shard_map.104 = (bf16[8,32,384]{2,1,0:T(8,128)(2,1)S(1)}, s32[8,8,128]{2,1,0:T(8,128)S(1)}) custom-call(bf16[32,384]{1,0:T(8,128)(2,1)S(1)} %copy-done.1, s32[8,128]{1,0:T(8,128)S(1)} %broadcast_in_dim.4.refs_1_), custom_call_target="tpu_custom_call" | custom-call | tf_op jit(solution)/shard_map/pallas_call | solution.py:200
  23.6 0.2 broadcast_in_dim_reshape.3.low_ref
  23.8 2.1 %fusion.17.refs_2_ = bf16[4,256,512]{2,1,0:T(8,128)(2,1)S(1)} fusion(bf16[256,384,1]{1,0,2:T(8,128)(2,1)S(1)} %bitcast.70, bf16[4,432,384]{2,1,0:T(8,128)(2,1)} %bitcast.73), kind=kOutput, calls=%fused_computation.25 | convolution fusion | flops 403177472 | bytes 2572288 | tf_op jit(solution)/shard_map/fc,mkc->mfk/dot_general | solution.py:405
  25.9 14.4 %shard_map.105 = (bf16[8,288,128]{2,1,0:T(8,128)(2,1)S(1)}, bf16[8,144,128]{2,1,0:T(8,128)(2,1)S(1)}, bf16[256,512]{1,0:T(8,128)(2,1)S(1)}) custom-call(bf16[6,288,128]{2,1,0:T(8,128)(2,1)S(1)} %maximum_bitcast_fusion.refs_0_, bf16[6,144,128]{2,1,0:T(8,128)(2,1)S(1)} %maximum_bitcast_fusion.1.refs_1_, bf16[4,256,512]{2,1,0:T(8,128)(2,1)S(1)} %fusion.17.refs_2_), custom_call_target="tpu_custom_call" | custom-call | tf_op jit(solution)/shard_map/pallas_call | solution.py:200
  40.3 31.0 %shard_map.107 = (bf16[6,144,128]{2,1,0:T(8,128)(2,1)S(1)}, bf16[8,32,512]{2,1,0:T(8,128)(2,1)S(1)}) custom-call(bf16[8,144,128]{2,1,0:T(8,128)(2,1)S(1)} %get-tuple-element.30.refs_0_, bf16[8,32,512]{2,1,0:T(8,128)(2,1)S(1)} %bitcast.68), custom_call_target="tpu_custom_call" | custom-call | tf_op jit(solution)/shard_map/pallas_call | solution.py:200
  71.3 0.7 fusion.44
  72.0 1.8 copy.22
  73.8 0.8 copy.23
  74.7 3.0 %fusion = bf16[288,1536]{1,0:T(8,128)(2,1)} fusion(bf16[384,1536]{1,0:T(8,128)(2,1)S(1)} %copy-done, bf16[288,1536]{1,0:T(8,128)(2,1)} %param.9, bf16[144,384]{0,1:T(8,128)(2,1)} %bitcast.86, bf16[144,384]{0,1:T(8,128)(2,1)} %bitcast.85), kind=kOutput, calls=%fused_computation.8 | convolution fusion | flops 341950464 | bytes 3170304 | tf_op jit(solution)/shard_map/dot_general | solution.py:447
  77.7 4.5 %reshape.109 = bf16[32,8,4,432]{3,2,1,0:T(4,128)(2,1)} reshape(bf16[288,1536]{1,0:T(8,128)(2,1)} %fusion) | data formatting | bytes 1769472 | tf_op jit(solution)/shard_map/reshape | solution.py:448
  82.2 1.8 copy.24
  84.2 16.2 %shard_map.108 = (bf16[4,8,32,512]{3,2,1,0:T(8,128)(2,1)S(1)}, bf16[256,512]{1,0:T(8,128)(2,1)S(1)}) custom-call(bf16[8,32,512]{2,1,0:T(8,128)(2,1)S(1)} %get-tuple-element.32.refs_0_, bf16[4,256,512]{2,1,0:T(8,128)(2,1)S(1)} %bitcast.60), custom_call_target="tpu_custom_call" | custom-call | tf_op jit(solution)/shard_map/pallas_call | solution.py:200
  100.5 1.8 copy.25
  102.2 4.0 %reshape.111 = bf16[288,1536]{1,0:T(8,128)(2,1)} reshape(bf16[32,8,4,432]{3,2,1,0:T(4,128)(2,1)} %copy.25) | data formatting | bytes 1769472 | tf_op jit(solution)/shard_map/reshape | solution.py:452
  106.2 1.8 convolution_convert_fusion
  108.0 0.7 fusion.43
  108.7 0.8 copy.26
  109.5 1.1 copy.28
  110.6 1.7 copy.27
  112.3 1.8 copy.29
  114.1 1.1 maximum_bitcast_fusion.2.refs_0_
  115.2 13.5 %shard_map.109 = (bf16[8,144,128]{2,1,0:T(8,128)(2,1)S(1)}, bf16[8,32,512]{2,1,0:T(8,128)(2,1)S(1)}) custom-call(bf16[6,144,128]{2,1,0:T(8,128)(2,1)S(1)} %maximum_bitcast_fusion.2.refs_0_, bf16[8,32,512]{2,1,0:T(8,128)(2,1)S(1)} %bitcast.69), custom_call_target="tpu_custom_call" | custom-call | tf_op jit(solution)/shard_map/pallas_call | solution.py:200
  128.7 35.4 %shard_map.111 = (bf16[6,144,128]{2,1,0:T(8,128)(2,1)S(1)}, bf16[6,288,128]{2,1,0:T(8,128)(2,1)S(1)}, bf16[4,8,32,512]{3,2,1,0:T(8,128)(2,1)S(1)}) custom-call(bf16[8,144,128]{2,1,0:T(8,128)(2,1)S(1)} %get-tuple-element.40.refs_0_, bf16[8,288,128]{2,1,0:T(8,128)(2,1)S(1)} %bitcast.67, bf16[8,32,512]{2,1,0:T(8,128)(2,1)S(1)} %get-tuple-element.42.refs_2_), custom_call_target="tpu_custom_call" | custom-call | tf_op jit(solution)/shard_map/pallas_call | solution.py:200
  164.1 0.7 fusion.23
  165.3 0.2 fusion.41
  165.5 0.3 copy.33
  165.7 0.3 copy.32
  166.0 2.2 %fusion.30 = f32[288,1536]{1,0:T(8,128)S(1)} fusion(bf16[1536,384]{1,0:T(8,128)(2,1)} %param.11, bf16[144,384]{0,1:T(8,128)(2,1)S(1)} %bitcast.80, bf16[144,384]{0,1:T(8,128)(2,1)S(1)} %bitcast.79), kind=kOutput, calls=%fused_computation.38 | convolution fusion | flops 340180992 | bytes 3170304 | tf_op jit(solution)/shard_map/dot_general | solution.py:30
  168.2 0.7 convolution_add_fusion.1
  169.0 0.5 copy-done.6
  169.5 0.7 fusion.1
  170.2 14.0 %shard_map.112 = (bf16[72,1536]{1,0:T(8,128)(2,1)S(1)}, bf16[8,32,384]{2,1,0:T(8,128)(2,1)S(1)}) custom-call(bf16[4,72,1536]{2,1,0:T(8,128)(2,1)S(1)} %bitcast.61, bf16[8,32,384]{2,1,0:T(8,128)(2,1)S(1)} %bitcast.71), custom_call_target="tpu_custom_call" | custom-call | tf_op jit(solution)/shard_map/pallas_call | solution.py:200
  184.2 0.6 reduce_sum.31
  184.8 9.4 %shard_map.113 = bf16[4,72,1536]{2,1,0:T(8,128)(2,1)S(1)} custom-call(bf16[72,1536]{1,0:T(8,128)(2,1)S(1)} %get-tuple-element.47.refs_0_), custom_call_target="tpu_custom_call" | custom-call | tf_op jit(solution)/shard_map/pallas_call | solution.py:200
  194.2 0.4 fusion.9
  194.6 2.7 %fusion.4 = bf16[288,1536]{1,0:T(8,128)(2,1)} fusion(bf16[288,1536]{1,0:T(8,128)(2,1)S(1)} %copy-done.3, bf16[288,1536]{1,0:T(8,128)(2,1)} %reshape.111, bf16[4,72,1536]{2,1,0:T(8,128)(2,1)S(1)} %shard_map.113, f32[288]{0:T(512)S(1)} %broadcast_multiply_fusion, f32[288]{0:T(512)S(1)} %get-tuple-element.58, f32[1536]{0:T(1024)S(1)} %copy-done.7, ...), kind=kLoop, calls=%fused_computation.14 | loop fusion | flops 4423680 | bytes 3548544 | tf_op jit(solution)/shard_map/convert_element_type | solution.py:496
  (32 shorter events, 1.4 us)
Async XLA Ops:
  0.6 74.0 %copy-start = (bf16[384,1536]{1,0:T(8,128)(2,1)S(1)}, bf16[384,1536]{1,0:T(8,128)(2,1)}, u32[]{:S(2)}) copy-start(bf16[384,1536]{1,0:T(8,128)(2,1)} %param.14) | copy-start | bytes 3538948
  2.9 2.8 %copy-start.2 = (bf16[288,1536]{1,0:T(8,128)(2,1)S(1)}, bf16[288,1536]{1,0:T(8,128)(2,1)}, u32[]{:S(2)}) copy-start(bf16[288,1536]{1,0:T(8,128)(2,1)} %param.9) | copy-start | bytes 2654212
  2.9 2.8 %copy-start.7 = (f32[1536]{0:T(1024)S(1)}, f32[1536]{0:T(1024)}, u32[]{:S(2)}) copy-start(f32[1536]{0:T(1024)} %param.10) | copy-start | bytes 18436
  10.5 0.8 copy-start.1
  115.1 49.0 %copy-start.4 = (bf16[1728,384]{1,0:T(8,128)(2,1)S(1)}, bf16[1728,384]{1,0:T(8,128)(2,1)}, u32[]{:S(2)}) copy-start(bf16[1728,384]{1,0:T(8,128)(2,1)} %param.15) | copy-start | bytes 3981316
  166.0 2.2 %copy-start.5 = (bf16[1536,384]{1,0:T(8,128)(2,1)S(1)}, bf16[1536,384]{1,0:T(8,128)(2,1)}, u32[]{:S(2)}) copy-start(bf16[1536,384]{1,0:T(8,128)(2,1)} %param.12) | copy-start | bytes 3538948
  168.2 1.3 copy-start.6
  170.2 24.0 %copy-start.3 = (bf16[288,1536]{1,0:T(8,128)(2,1)S(1)}, bf16[288,1536]{1,0:T(8,128)(2,1)}, u32[]{:S(2)}) copy-start(bf16[288,1536]{1,0:T(8,128)(2,1)} %param.9) | copy-start | bytes 2654212

commit v3 on v2

--- a/solution.py
+++ b/solution.py
@@ -358,25 +358,58 @@
     )(*arrays)
 
 
-def by_heads(left, right):
-    rows = left.shape[0]
-    pair = [part.reshape(rows, -1, HEAD) for part in (left, right)]
-    return jnp.concatenate(pair, axis=2).transpose(1, 0, 2)
-
-
-def packed_heads(array):
-    half = array.shape[0] // 2
-    return by_heads(array[:half], array[half:])
-
-
-def from_heads(pair):
-    rows = pair.shape[1]
-    flat = pair.transpose(1, 0, 2)
-    return flat[:, :, :HEAD].reshape(rows, -1), flat[:, :, HEAD:].reshape(rows, -1)
-
-
-def unpacked_heads(pair):
-    return jnp.concatenate(from_heads(pair), axis=0)
+def twist(left, right):
+    low_half = lax.broadcasted_iota(jnp.int32, left.shape, 1) < HEAD
+    first = jnp.where(low_half, left, rolled(right).astype(left.dtype))
+    second = jnp.where(low_half, rolled(left).astype(left.dtype), right)
+    return first, second
+
+
+def split_pairs(left, right, out_ref):
+    for pair in range(left.shape[1] // LANES):
+        lanes = slice(pair * LANES, (pair + 1) * LANES)
+        out_ref[2 * pair], out_ref[2 * pair + 1] = twist(left[:, lanes], right[:, lanes])
+
+
+def join_pairs(ref):
+    lefts, rights = zip(*(twist(ref[head], ref[head + 1]) for head in range(0, ref.shape[0], 2)))
+    return jnp.concatenate(lefts, axis=1), jnp.concatenate(rights, axis=1)
+
+
+def rounded_dot(left, right):
+    return jnp.dot(left, right, preferred_element_type=jnp.float32).astype(jnp.bfloat16)
+
+
+def prepare_kernel(x_ref, gain_ref, wq_ref, wk_ref, wv_ref, kv_ref, packed_ref):
+    x = x_ref[...].astype(jnp.float32)
+    scale_r = lax.rsqrt(jnp.mean(x * x, axis=-1, keepdims=True) + 1e-05)
+    normed = (x * scale_r * gain_ref[...]).astype(jnp.bfloat16)
+    split_pairs(rounded_dot(normed, wk_ref[...]), rounded_dot(normed, wv_ref[...]), kv_ref)
+    query = rounded_dot(normed, wq_ref[...]) * jnp.bfloat16(HEAD ** (-0.5))
+    half = query.shape[0] // 2
+    split_pairs(query[:half], query[half:], packed_ref)
+
+
+def project_kernel(parts, packed_ref, w_ref, x_ref, out_ref):
+    top, bottom = join_pairs(packed_ref)
+    half = top.shape[0]
+    for rows, part in ((slice(0, half), top), (slice(half, 2 * half), bottom)):
+        product = jnp.dot(part, w_ref[...], preferred_element_type=jnp.float32)
+        x = x_ref[rows, :].astype(jnp.float32) * (1.0 / parts)
+        out_ref[rows, :] = (product + x).astype(jnp.bfloat16)
+
+
+def d_attended_kernel(d_mixed_ref, w_ref, packed_ref):
+    d_attended = times_rows(d_mixed_ref[...], w_ref[...]).astype(jnp.bfloat16)
+    half = d_attended.shape[0] // 2
+    split_pairs(d_attended[:half], d_attended[half:], packed_ref)
+
+
+def d_normed_kernel(dq_ref, dkv_ref, wq_ref, wk_ref, wv_ref, out_ref):
+    d_query = jnp.concatenate(join_pairs(dq_ref), axis=0)
+    d_key, d_value = join_pairs(dkv_ref)
+    total = times_rows(d_query, wq_ref[...]) + times_rows(d_key, wk_ref[...])
+    out_ref[...] = (total + times_rows(d_value, wv_ref[...])).astype(jnp.bfloat16)
 
 
 def by_head_owner(
@@ -384,9 +417,12 @@
 ):
     tok_rows, model_width = tokens.shape
     face_rows = tok_rows // 9
-    heads = w_query.shape[1] // HEAD
+    width = w_query.shape[1]
+    heads = width // HEAD
     seq_count, mp_count = lax.axis_size("seq"), lax.axis_size("mp")
-    chunk = w_shorten.shape[0] // mp_count
+    share = face_rows // mp_count
+    halves = 16 // share
+    chunk = w_shorten.shape[0] // halves
     padded = -(-chunk // 128) * 128
     tok_total = tok_rows * seq_count
     faces_total = face_rows * seq_count
@@ -400,27 +436,30 @@
     low = jnp.repeat(all_bounds[:, 0, :face_rows].reshape(faces_total), 9)[None]
 
     shorten = jnp.pad(
-        w_shorten.reshape(mp_count, chunk, -1), ((0, 0), (0, padded - chunk), (0, 0))
-    )
-    d_partial = jnp.einsum(
-        "fc,mkc->mfk",
-        all_d_faces.reshape(faces_total, -1),
-        shorten,
-        preferred_element_type=f32,
-    ).astype(bf16)
-
-    x_float = tokens.astype(f32)
-    scale_r = lax.rsqrt(jnp.mean(x_float * x_float, axis=-1, keepdims=True) + 1e-05)
-    normed = (x_float * scale_r * norm_gain).astype(bf16)
-    query = jnp.dot(normed, w_query, preferred_element_type=f32).astype(bf16)
-    key = jnp.dot(normed, w_key, preferred_element_type=f32).astype(bf16)
-    value = jnp.dot(normed, w_value, preferred_element_type=f32).astype(bf16)
-
+        w_shorten.reshape(halves, chunk, -1), ((0, 0), (0, padded - chunk), (0, 0))
+    )
+    by_share = all_d_faces.reshape(seq_count, mp_count, share, -1).transpose(1, 0, 2, 3)
+    by_share = by_share.reshape(faces_total, -1)
+    d_partial = [
+        times_rows(by_share, shorten[half])
+        .astype(bf16)
+        .reshape(mp_count, seq_count, share, padded)
+        for half in range(halves)
+    ]
+    d_partial = jnp.concatenate(d_partial, axis=2)
+    d_partial = d_partial.reshape(mp_count, seq_count * halves * share, padded)
+
+    half_rows = tok_rows // 2
+    kv, packed_query = plain_call(
+        prepare_kernel,
+        (tokens, norm_gain[None], w_query, w_key, w_value),
+        (((heads, tok_rows, LANES), bf16), ((heads, half_rows, LANES), bf16)),
+    )
     kv, packed_query, d_chunk = exchange(
         2,
         [
-            (by_heads(key, value), "seq", "to_heads"),
-            (packed_heads(query * bf16(HEAD ** (-0.5))), "seq", "to_heads"),
+            (kv, "seq", "to_heads"),
+            (packed_query, "seq", "to_heads"),
             (d_partial, "mp", "reduce"),
         ],
         heads,
@@ -428,36 +467,41 @@
     kv = kv.reshape(tok_total, LANES)
     tile, span = tiling(tok_total)
     flat = ((tok_total, LANES), bf16)
-    folded = ((seq_count, tok_rows // 2, LANES), bf16)
+    folded = ((seq_count, half_rows, LANES), bf16)
     line = ((1, tok_total), f32)
     att_packed, query_flat, att_flat, top, inverse = plain_call(
         functools.partial(forward_kernel, heads, tile, span),
         (kv, packed_query, low),
         (folded, flat, flat, line, line),
     )
+    moved = (seq_count, halves * share, padded)
     att_packed, d_chunk = exchange(
         3,
+        [(att_packed, "seq", "from_heads"), (d_chunk.reshape(moved), "seq", "all")],
+        heads,
+    )
+    (projected,) = plain_call(
+        functools.partial(project_kernel, mp_count),
+        (att_packed, w_out, tokens),
+        [((tok_rows, model_width), bf16)],
+    )
+    d_chunk = d_chunk.reshape(seq_count, halves, share, padded)[..., :chunk]
+    d_chunk = d_chunk.transpose(2, 0, 1, 3).reshape(tok_rows // mp_count, model_width)
+    d_mixed, mixed = exchange(
+        4,
         [
-            (att_packed, "seq", "from_heads"),
-            (d_chunk.reshape(seq_count, face_rows, padded), "seq", "all"),
+            (d_chunk, "mp", "gather"),
+            (projected.reshape(mp_count, *d_chunk.shape), "mp", "reduce"),
         ],
-        heads,
-    )
-    attended = unpacked_heads(att_packed)
-    projected = jnp.dot(attended, w_out, preferred_element_type=f32) + x_float / mp_count
-    projected = projected.astype(bf16).reshape(face_rows, seq_count, mp_count, chunk)
-    projected = jnp.pad(projected, ((0, 0), (0, 0), (0, 0), (0, padded - chunk)))
-    projected = projected.transpose(2, 1, 0, 3).reshape(mp_count, faces_total, padded)
-    d_whole, mixed = exchange(4, [(d_chunk, "mp", "gather"), (projected, "mp", "reduce")])
-    d_mixed = d_whole[..., :chunk].transpose(2, 1, 0, 3).reshape(tok_rows, model_width)
-    d_attended = times_rows(d_mixed, w_out).astype(bf16)
+    )
+    d_mixed = d_mixed.reshape(tok_rows, model_width)
+    (d_att_packed,) = plain_call(
+        d_attended_kernel, (d_mixed, w_out), [((heads, half_rows, LANES), bf16)]
+    )
+    mixed = mixed.reshape(share, seq_count, halves, chunk).transpose(1, 2, 0, 3)
+    mixed = jnp.pad(mixed, ((0, 0), (0, 0), (0, 0), (0, padded - chunk))).reshape(moved)
     d_att_packed, mixed = exchange(
-        5,
-        [
-            (packed_heads(d_attended), "seq", "to_heads"),
-            (mixed.reshape(seq_count, face_rows, padded), "seq", "all"),
-        ],
-        heads,
+        5, [(d_att_packed, "seq", "to_heads"), (mixed, "seq", "all")], heads
     )
     d_query, d_kv = plain_call(
         functools.partial(backward_kernel, heads, tile, span),
@@ -474,25 +518,34 @@
         ],
         heads,
     )
-    partial = jnp.einsum(
-        "mfk,mkc->fc",
-        mixed.reshape(mp_count, faces_total, padded),
-        shorten,
-        preferred_element_type=f32,
-    )
-    partial = partial.astype(bf16).reshape(seq_count, face_rows, -1)
-    d_query = unpacked_heads(d_query)
-    d_key, d_value = from_heads(d_kv)
-    part_normed = times_rows(d_query, w_query)
-    part_normed = part_normed + times_rows(d_key, w_key)
-    part_normed = part_normed + times_rows(d_value, w_value)
-    part_normed = part_normed.astype(bf16).reshape(mp_count, tok_rows // mp_count, model_width)
+    (part_normed,) = plain_call(
+        d_normed_kernel,
+        (d_query, d_kv, w_query, w_key, w_value),
+        [((tok_rows, model_width), bf16)],
+    )
+    mixed = mixed.reshape(mp_count, seq_count, halves, share, padded)
+    partial = sum(
+        jnp.dot(
+            mixed[:, :, half].reshape(faces_total, padded),
+            shorten[half],
+            preferred_element_type=f32,
+        )
+        for half in range(halves)
+    )
+    partial = partial.astype(bf16).reshape(mp_count, seq_count, share, -1)
+    partial = partial.transpose(1, 0, 2, 3).reshape(seq_count, face_rows, -1)
     part_normed, partial = exchange(
-        7, [(part_normed, "mp", "reduce"), (partial, "seq", "all")]
+        7,
+        [
+            (part_normed.reshape(mp_count, *d_chunk.shape), "mp", "reduce"),
+            (partial, "seq", "all"),
+        ],
     )
     (d_normed,) = exchange(8, [(part_normed, "mp", "gather")])
     faces = jnp.sum(partial.astype(f32), axis=0).astype(bf16)
     d_normed = d_normed.reshape(tok_rows, model_width).astype(f32)
+    x_float = tokens.astype(f32)
+    scale_r = lax.rsqrt(jnp.mean(x_float * x_float, axis=-1, keepdims=True) + 1e-05)
     d_tokens = finish(d_normed, x_float, scale_r, d_mixed, norm_gain).astype(bf16)
     return (faces, d_tokens)
 
@@ -614,7 +667,8 @@
 def local(*arrays):
     heads = arrays[2].shape[1] // HEAD
     seq_count = lax.axis_size("seq")
-    if heads <= seq_count < 2 * heads and lax.axis_size("mp") == 4:
+    whole_pairs = heads % 2 == 0 and lax.axis_size("mp") == 4
+    if heads <= seq_count < 2 * heads and whole_pairs:
         return by_head_owner(*arrays)
     return by_window(*arrays)
 

time: 198 us -> 173 us (0.87)
  matrix products: 17.4 us -> 4.16 us
  local copies, waits for them, and re-layouts: 26.3 us -> 16.5 us
  other arithmetic: 6.63 us -> 2.77 us
  Pallas kernels: 146 us -> 148 us
    reshape x9 -> x6, local copies, waits for them, and re-layouts: 14.1 us -> 2.83 us  [the longest x2 1.42 us: by_head_owner(): mixed = mixed.reshape(share, seq_count, halves, chunk).transpose(1, 2, 0, 3)]
    dot_general x6 -> x2, matrix products: 12 us -> 0.8 us  [by_head_owner(): jnp.dot(mixed[:, :, half].reshape(faces_total, padded), shorten[half], pr...]
    unnamed x16 -> x45, local copies, waits for them, and re-layouts: 0.6 us -> 11.8 us
    slice x15 -> x1, local copies, waits for them, and re-layouts: 7.99 us -> 0.11 us  [by_head_owner(): mixed[:, :, half].reshape(faces_total, padded)]
    pallas_call x2 -> x6, Pallas kernels: 0.04 us -> 4.78 us  [plain_call(): pl.pallas_call(body, out_shape=[jax.ShapeDtypeStruct(*shape) for shape in...]
    pallas_call x8, Pallas kernels: 146 us -> 143 us  [exchange(): pl.pallas_call(functools.partial(exchange_kernel, tuple(plan), heads, fir...]
    dot_general x4 -> x2, matrix products: 5.42 us -> 3.36 us  [times_rows(): lax.dot_general(left, right, (((1,), (1,)), ((), ())), preferred_element_...]
where the time goes in v3:
time: 173 us; the launch traced here: 172 us
  Pallas kernels  148 us (86%)
  local copies, waits for them, and re-layouts  16.5 us (10%)
  matrix products  4.16 us (2%)
  other arithmetic  2.77 us (2%)
    pallas_call x8, Pallas kernels, exchange(): pl.pallas_call(functools.partial(exchange_kernel, tuple(plan), heads, fir...  143 us
    unnamed x45, local copies, waits for them, and re-layouts  11.8 us
    pallas_call x6, Pallas kernels, plain_call(): pl.pallas_call(body, out_shape=[jax.ShapeDtypeStruct(*shape) for shape in...  4.78 us

profile of v3, /device:TPU:0, one launch (start us, length us, event | category | flops | bytes accessed | tf_op | source)
XLA Modules:
  0.0 172.4 jit_solution(3346778484541958246)
XLA Ops:
  0.6 0.7 pad.12
  1.3 0.7 broadcast_in_dim.6.gain_ref
  2.0 0.7 copy-done.19
  2.7 12.0 %shard_map.105 = (bf16[8,32,384]{2,1,0:T(8,128)(2,1)S(1)}, s32[8,8,128]{2,1,0:T(8,128)S(1)}) custom-call(bf16[32,384]{1,0:T(8,128)(2,1)S(1)} %copy-done.19, s32[8,128]{1,0:T(8,128)S(1)} %broadcast_in_dim.7.refs_1_), custom_call_target="tpu_custom_call" | custom-call | tf_op jit(solution)/shard_map/pallas_call | solution.py:200
  14.8 0.1 reshape_squeeze.9
  14.9 0.1 broadcast_in_dim.8
  15.0 0.2 broadcast_in_dim_reshape.3.low_ref
  15.2 0.0 copy-start.3
  15.2 1.7 convolution_convert_fusion
  16.9 0.0 copy-start.1
  16.9 0.0 copy-start.2
  16.9 1.7 convolution_convert_fusion.1
  18.6 0.0 copy-start
  18.6 0.1 pad_maximum_fusion
  18.8 1.1 copy-done
  19.8 1.8 %shard_map.104 = (bf16[6,288,128]{2,1,0:T(8,128)(2,1)S(1)}, bf16[6,144,128]{2,1,0:T(8,128)(2,1)S(1)}) custom-call(bf16[288,1536]{1,0:T(8,128)(2,1)S(1)} %copy-done, f32[1,1536]{1,0:T(1,128)S(1)} %broadcast_in_dim.6.gain_ref, bf16[1536,384]{1,0:T(8,128)(2,1)S(1)} %copy-done.1, bf16[1536,384]{1,0:T(8,128)(2,1)S(1)} %copy-done.2, bf16[1536,384]{1,0:T(8,128)(2,1)S(1)} %copy-done.3), custom_call_target="tpu_custom_call" | custom-call | tf_op jit(solution)/shard_map/pallas_call | solution.py:351
  21.6 14.5 %shard_map.106 = (bf16[8,288,128]{2,1,0:T(8,128)(2,1)S(1)}, bf16[8,144,128]{2,1,0:T(8,128)(2,1)S(1)}, bf16[128,896]{1,0:T(8,128)(2,1)S(1)}) custom-call(bf16[6,288,128]{2,1,0:T(8,128)(2,1)S(1)} %get-tuple-element.27.refs_0_, bf16[6,144,128]{2,1,0:T(8,128)(2,1)S(1)} %get-tuple-element.28.refs_1_, bf16[4,128,896]{2,1,0:T(8,128)(2,1)S(1)} %bitcast.50), custom_call_target="tpu_custom_call" | custom-call | tf_op jit(solution)/shard_map/pallas_call | solution.py:200
  36.1 0.8 copy-done.10
  37.0 0.8 copy-done.14
  37.8 30.4 %shard_map.108 = (bf16[6,144,128]{2,1,0:T(8,128)(2,1)S(1)}, bf16[8,16,896]{2,1,0:T(8,128)(2,1)S(1)}) custom-call(bf16[8,144,128]{2,1,0:T(8,128)(2,1)S(1)} %get-tuple-element.34.refs_0_, bf16[8,16,896]{2,1,0:T(8,128)(2,1)S(1)} %bitcast.60), custom_call_target="tpu_custom_call" | custom-call | tf_op jit(solution)/shard_map/pallas_call | solution.py:200
  68.2 0.9 copy.22
  69.1 1.3 reshape.93.refs_0_
  70.5 0.0 copy-start.5
  70.5 1.3 copy-done.5
  71.7 0.9 copy-done.17
  72.7 0.7 shard_map.109
  73.3 14.6 %shard_map.110 = (bf16[4,72,1536]{2,1,0:T(8,128)(2,1)S(1)}, bf16[72,1536]{1,0:T(8,128)(2,1)S(1)}) custom-call(bf16[72,1536]{1,0:T(8,128)(2,1)S(1)} %reshape.93.refs_0_, bf16[4,72,1536]{2,1,0:T(8,128)(2,1)S(1)} %bitcast.52), custom_call_target="tpu_custom_call" | custom-call | tf_op jit(solution)/shard_map/pallas_call | solution.py:200
  88.0 0.0 copy-start.7
  88.0 0.9 copy-done.7
  88.9 0.7 copy-done.18
  89.6 1.4 reshape.96
  91.1 1.1 copy-done.8
  92.1 1.3 copy-done.6
  93.4 0.7 shard_map.111.refs_0_
  94.1 13.0 %shard_map.112 = (bf16[8,144,128]{2,1,0:T(8,128)(2,1)S(1)}, bf16[8,16,896]{2,1,0:T(8,128)(2,1)S(1)}) custom-call(bf16[6,144,128]{2,1,0:T(8,128)(2,1)S(1)} %shard_map.111.refs_0_, bf16[8,16,896]{2,1,0:T(8,128)(2,1)S(1)} %pad_bitcast_fusion.refs_1_), custom_call_target="tpu_custom_call" | custom-call | tf_op jit(solution)/shard_map/pallas_call | solution.py:200
  107.2 0.0 copy-start.4
  107.2 36.4 %shard_map.114 = (bf16[6,144,128]{2,1,0:T(8,128)(2,1)S(1)}, bf16[6,288,128]{2,1,0:T(8,128)(2,1)S(1)}, bf16[4,8,16,896]{3,2,1,0:T(8,128)(2,1)S(1)}) custom-call(bf16[8,144,128]{2,1,0:T(8,128)(2,1)S(1)} %get-tuple-element.44.refs_0_, bf16[8,288,128]{2,1,0:T(8,128)(2,1)S(1)} %bitcast.58, bf16[8,16,896]{2,1,0:T(8,128)(2,1)S(1)} %get-tuple-element.46.refs_2_), custom_call_target="tpu_custom_call" | custom-call | tf_op jit(solution)/shard_map/pallas_call | solution.py:200
  143.6 1.6 shard_map.115
  145.2 0.0 copy-start.20
  145.2 0.1 fusion.18
  145.4 1.2 copy-done.20
  146.5 0.4 fusion.11
  147.0 0.4 fusion.6
  147.4 12.9 %shard_map.116 = (bf16[72,1536]{1,0:T(8,128)(2,1)S(1)}, bf16[8,32,384]{2,1,0:T(8,128)(2,1)S(1)}) custom-call(bf16[4,72,1536]{2,1,0:T(8,128)(2,1)S(1)} %bitcast.51, bf16[8,32,384]{2,1,0:T(8,128)(2,1)S(1)} %bitcast.57), custom_call_target="tpu_custom_call" | custom-call | tf_op jit(solution)/shard_map/pallas_call | solution.py:200
  160.3 0.6 reduce_sum.30
  160.9 9.4 %shard_map.117 = bf16[4,72,1536]{2,1,0:T(8,128)(2,1)S(1)} custom-call(bf16[72,1536]{1,0:T(8,128)(2,1)S(1)} %get-tuple-element.51.refs_0_), custom_call_target="tpu_custom_call" | custom-call | tf_op jit(solution)/shard_map/pallas_call | solution.py:200
  170.3 0.5 fusion.3
  170.8 1.6 fusion.2
  (34 shorter events, 0.2 us)
Async XLA Ops:
  2.0 0.7 copy-start.19
  15.2 3.5 %copy-start.3 = (bf16[1536,384]{1,0:T(8,128)(2,1)S(1)}, bf16[1536,384]{1,0:T(8,128)(2,1)}, u32[]{:S(2)}) copy-start(bf16[1536,384]{1,0:T(8,128)(2,1)} %wv_ref.3) | copy-start | bytes 3538948
  16.9 1.8 %copy-start.1 = (bf16[1536,384]{1,0:T(8,128)(2,1)S(1)}, bf16[1536,384]{1,0:T(8,128)(2,1)}, u32[]{:S(2)}) copy-start(bf16[1536,384]{1,0:T(8,128)(2,1)} %wq_ref.3) | copy-start | bytes 3538948
  16.9 1.8 %copy-start.2 = (bf16[1536,384]{1,0:T(8,128)(2,1)S(1)}, bf16[1536,384]{1,0:T(8,128)(2,1)}, u32[]{:S(2)}) copy-start(bf16[1536,384]{1,0:T(8,128)(2,1)} %wk_ref.3) | copy-start | bytes 3538948
  18.6 1.2 copy-start
  36.1 0.8 copy-start.10
  37.0 0.8 copy-start.14
  37.8 31.3 %copy-start.12 = (bf16[2304,128]{1,0:T(8,128)(2,1)}, bf16[2304,128]{1,0:T(8,128)(2,1)S(1)}, u32[]{:S(2)}) copy-start(bf16[2304,128]{1,0:T(8,128)(2,1)S(1)} %get-tuple-element.33.query_ref) | copy-start | bytes 1769476
  68.2 0.9 copy-start.16
  70.5 1.3 copy-start.5
  71.7 0.9 copy-start.17
  88.0 0.9 copy-start.7
  88.9 0.7 copy-start.18
  91.0 1.2 copy-start.8
  92.1 1.3 copy-start.6
  93.4 13.7 %copy-start.11 = (bf16[8,288,128]{2,1,0:T(8,128)(2,1)S(1)}, bf16[8,288,128]{2,1,0:T(8,128)(2,1)}, u32[]{:S(2)}) copy-start(bf16[8,288,128]{2,1,0:T(8,128)(2,1)} %copy-done.10) | copy-start | bytes 1769476
  93.4 13.7 %copy-start.13 = (bf16[2304,128]{1,0:T(8,128)(2,1)S(1)}, bf16[2304,128]{1,0:T(8,128)(2,1)}, u32[]{:S(2)}) copy-start(bf16[2304,128]{1,0:T(8,128)(2,1)} %copy-done.12) | copy-start | bytes 1769476
  93.4 13.7 %copy-start.15 = (bf16[2304,128]{1,0:T(8,128)(2,1)S(1)}, bf16[2304,128]{1,0:T(8,128)(2,1)}, u32[]{:S(2)}) copy-start(bf16[2304,128]{1,0:T(8,128)(2,1)} %copy-done.14) | copy-start | bytes 1769476
  107.2 36.5 %copy-start.4 = (bf16[1536,384]{1,0:T(8,128)(2,1)S(1)}, bf16[1536,384]{1,0:T(8,128)(2,1)}, u32[]{:S(2)}) copy-start(bf16[1536,384]{1,0:T(8,128)(2,1)} %wv_ref.3) | copy-start | bytes 3538948
  145.2 1.3 copy-start.20
  147.4 22.9 %copy-start.21 = (f32[1536]{0:T(1024)S(1)}, f32[1536]{0:T(1024)}, u32[]{:S(2)}) copy-start(f32[1536]{0:T(1024)} %param.10) | copy-start | bytes 18436
  160.9 9.9 %copy-start.9 = (bf16[4,72,1536]{2,1,0:T(8,128)(2,1)S(1)}, bf16[4,72,1536]{2,1,0:T(8,128)(2,1)}, u32[]{:S(2)}) copy-start(bf16[4,72,1536]{2,1,0:T(8,128)(2,1)} %copy-done.7) | copy-start | bytes 2654212

commit v4 on v3

--- a/solution.py
+++ b/solution.py
@@ -237,10 +237,10 @@
             flat_ref[pl.ds((2 * block + place) * half, half), :] = part
 
 
-def pack(flat_ref, packed_ref, upper):
+def pack(flat_ref, packed_ref, upper, chosen=None):
     blocks, half, _ = packed_ref.shape
     low_half = lax.broadcasted_iota(jnp.int32, (half, LANES), 1) < HEAD
-    for block in range(blocks):
+    for block in range(blocks) if chosen is None else chosen:
         top = flat_ref[pl.ds(2 * block * half, half), :]
         bottom = flat_ref[pl.ds((2 * block + 1) * half, half), :]
         if upper:
@@ -259,8 +259,58 @@
 
 
 def forward_kernel(
-    heads, tile, span, kv_ref, packed_ref, low_ref, out_ref, query_ref, att_ref, top_ref, inv_ref
+    heads, tile, span, kv_ref, packed_ref, low_ref, chunk_ref,
+    query_ref, att_ref, top_ref, inv_ref, att_out, chunk_out, att_packed,
+    att_send, att_recv, chunk_send, chunk_recv, own_sems,
 ):
+    size = lax.axis_size("seq")
+    first_owner = (size - heads) // 2
+    me = lax.axis_index("seq")
+    owner = (me >= first_owner) & (me < first_owner + heads)
+    barrier = pltpu.get_barrier_semaphore()
+    for step in range(1, size):
+        pl.semaphore_signal(
+            barrier,
+            inc=1,
+            device_id={"seq": lax.rem(me + step, size)},
+            device_id_type=pl.DeviceIdType.MESH,
+        )
+    pl.semaphore_wait(barrier, size - 1)
+
+    def remote(piece, slot, send_sem, recv_sem, peer):
+        return pltpu.make_async_remote_copy(
+            src_ref=piece,
+            dst_ref=slot,
+            send_sem=send_sem,
+            recv_sem=recv_sem,
+            device_id={"seq": peer},
+            device_id_type=pl.DeviceIdType.MESH,
+        )
+
+    chunk_copies = []
+    for step in range(1, size):
+        peer = lax.rem(me + step, size)
+        chunk_copies.append(
+            remote(
+                chunk_ref.at[peer], chunk_out.at[me], chunk_send.at[step], chunk_recv.at[step], peer
+            )
+        )
+    chunk_copies.append(
+        pltpu.make_async_copy(chunk_ref.at[me], chunk_out.at[me], own_sems.at[0])
+    )
+    for copy in chunk_copies:
+        copy.start()
+
+    att_slot = att_out.at[jnp.clip(me - first_owner, 0, heads - 1)]
+
+    def att_copy(block, origin):
+        return remote(
+            att_packed.at[block], att_slot, att_send.at[block], att_recv.at[origin], block
+        )
+
+    def own_copy(block):
+        return pltpu.make_async_copy(att_packed.at[block], att_slot, own_sems.at[1])
+
     def run():
         unpack(packed_ref, query_ref, False)
         high_half = lax.broadcasted_iota(jnp.int32, (tile, LANES), 1) >= HEAD
@@ -294,10 +344,54 @@
             att_ref[here, :] = jnp.where(high_half, attended, jnp.zeros_like(attended))
             return 0
 
-        lax.fori_loop(0, kv_ref.shape[0] // tile, query_step, 0)
-        pack(att_ref, out_ref, True)
-
-    when_owner(heads, run)
+        tiles = kv_ref.shape[0] // tile
+        rows = kv_ref.shape[0] // size
+        done = 0
+        for stop in range(span // tile, tiles + 1, span // tile):
+            lax.fori_loop(stop - span // tile, stop, query_step, 0)
+            ready = stop * tile // rows
+            pack(att_ref, att_packed, True, range(done, ready))
+            for block in range(done, ready):
+                pl.when(me != block)(att_copy(block, me).start)
+                pl.when(me == block)(own_copy(block).start)
+            done = ready
+        for block in range(size):
+            pl.when(me != block)(att_copy(block, me).wait_send)
+            pl.when(me == block)(own_copy(block).wait)
+
+    pl.when(owner)(run)
+    for origin in range(first_owner, first_owner + heads):
+        pl.when(me != origin)(att_copy(0, origin).wait_recv)
+    for copy in chunk_copies:
+        copy.wait()
+
+
+def forward(collective, heads, tile, span, kv, packed_query, low, d_chunk):
+    whole, anywhere = pl.BlockSpec(memory_space=pltpu.VMEM), pl.BlockSpec(memory_space=pl.ANY)
+    size = lax.axis_size("seq")
+    total = kv.shape[0]
+    flat = jax.ShapeDtypeStruct(kv.shape, jnp.bfloat16)
+    line = jax.ShapeDtypeStruct((1, total), jnp.float32)
+    half = packed_query.shape[1]
+    sems = pltpu.SemaphoreType.DMA((size,))
+    return pl.pallas_call(
+        functools.partial(forward_kernel, heads, tile, span),
+        out_shape=[
+            flat, flat, line, line,
+            jax.ShapeDtypeStruct((heads, half, LANES), jnp.bfloat16),
+            jax.ShapeDtypeStruct(d_chunk.shape, d_chunk.dtype),
+        ],
+        in_specs=[whole, whole, whole, anywhere],
+        out_specs=[whole] * 4 + [anywhere] * 2,
+        scratch_shapes=[
+            pltpu.VMEM((size, half, LANES), jnp.bfloat16),
+            sems, sems, sems, sems,
+            pltpu.SemaphoreType.DMA((2,)),
+        ],
+        compiler_params=pltpu.CompilerParams(
+            collective_id=collective, has_side_effects=True, vmem_limit_bytes=32 * 1024 * 1024
+        ),
+    )(kv, packed_query, low, d_chunk)
 
 
 def backward_kernel(
@@ -468,17 +562,9 @@
     tile, span = tiling(tok_total)
     flat = ((tok_total, LANES), bf16)
     folded = ((seq_count, half_rows, LANES), bf16)
-    line = ((1, tok_total), f32)
-    att_packed, query_flat, att_flat, top, inverse = plain_call(
-        functools.partial(forward_kernel, heads, tile, span),
-        (kv, packed_query, low),
-        (folded, flat, flat, line, line),
-    )
     moved = (seq_count, halves * share, padded)
-    att_packed, d_chunk = exchange(
-        3,
-        [(att_packed, "seq", "from_heads"), (d_chunk.reshape(moved), "seq", "all")],
-        heads,
+    query_flat, att_flat, top, inverse, att_packed, d_chunk = forward(
+        3, heads, tile, span, kv, packed_query, low, d_chunk.reshape(moved)
     )
     (projected,) = plain_call(
         functools.partial(project_kernel, mp_count),

time: 173 us -> 167 us (0.965)
  Pallas kernels: 148 us -> 141 us
    pallas_call x8 -> x7, Pallas kernels: 143 us -> 120 us  [exchange(): pl.pallas_call(functools.partial(exchange_kernel, tuple(plan), heads, fir...]
    pallas_call x0 -> x1, Pallas kernels: none -> 16.6 us  [forward(): pl.pallas_call(functools.partial(forward_kernel, heads, tile, span), out_...]
    pallas_call x6 -> x5, Pallas kernels: 4.78 us -> 4.76 us  [plain_call(): pl.pallas_call(body, out_shape=[jax.ShapeDtypeStruct(*shape) for shape in...]
where the time goes in v4:
time: 167 us
  Pallas kernels  141 us (84%)
  local copies, waits for them, and re-layouts  17.3 us (10%)
  matrix products  4.16 us (2%)
  other arithmetic  2.77 us (2%)
    pallas_call x7, Pallas kernels, exchange(): pl.pallas_call(functools.partial(exchange_kernel, tuple(plan), heads, fir...  120 us
    pallas_call x1, Pallas kernels, forward(): pl.pallas_call(functools.partial(forward_kernel, heads, tile, span), out_...  16.6 us
    unnamed x45, local copies, waits for them, and re-layouts  12.6 us
    pallas_call x5, Pallas kernels, plain_call(): pl.pallas_call(body, out_shape=[jax.ShapeDtypeStruct(*shape) for shape in...  4.76 us
    dot_general x2, matrix products, times_rows(): lax.dot_general(left, right, (((1,), (1,)), ((), ())), preferred_element_...  3.36 us

profile of v4, /device:TPU:0, one launch (start us, length us, event | category | flops | bytes accessed | tf_op | source)
XLA Modules:
  0.0 166.7 jit_solution(6177600089199209337)
XLA Ops:
  0.6 0.7 pad.12
  1.3 0.7 broadcast_in_dim.6.gain_ref
  2.0 0.7 copy-done.19
  2.7 12.0 %shard_map.105 = (bf16[8,32,384]{2,1,0:T(8,128)(2,1)S(1)}, s32[8,8,128]{2,1,0:T(8,128)S(1)}) custom-call(bf16[32,384]{1,0:T(8,128)(2,1)S(1)} %copy-done.19, s32[8,128]{1,0:T(8,128)S(1)} %broadcast_in_dim.7.refs_1_), custom_call_target="tpu_custom_call" | custom-call | tf_op jit(solution)/shard_map/pallas_call | solution.py:200
  14.8 0.1 reshape_squeeze.9
  14.9 0.1 broadcast_in_dim.8
  15.0 0.2 broadcast_in_dim_reshape.3.low_ref
  15.2 0.0 copy-start.3
  15.2 1.7 convolution_convert_fusion
  16.9 0.0 copy-start.1
  16.9 0.0 copy-start.2
  16.9 1.7 %convolution_convert_fusion.1 = bf16[256,896]{1,0:T(8,128)(2,1)S(1)} fusion(bf16[256,384]{1,0:T(8,128)(2,1)S(1)} %bitcast.71, bf16[2,864,384]{2,1,0:T(8,128)(2,1)} %bitcast.63), kind=kOutput, calls=%fused_computation.12 | convolution fusion | flops 176390144 | bytes 1982464 | tf_op jit(solution)/shard_map/dot_general | solution.py:30
  18.6 0.0 copy-start
  18.6 0.1 pad_maximum_fusion
  18.8 1.1 copy-done
  19.8 1.8 %shard_map.104 = (bf16[6,288,128]{2,1,0:T(8,128)(2,1)S(1)}, bf16[6,144,128]{2,1,0:T(8,128)(2,1)S(1)}) custom-call(bf16[288,1536]{1,0:T(8,128)(2,1)S(1)} %copy-done, f32[1,1536]{1,0:T(1,128)S(1)} %broadcast_in_dim.6.gain_ref, bf16[1536,384]{1,0:T(8,128)(2,1)S(1)} %copy-done.1, bf16[1536,384]{1,0:T(8,128)(2,1)S(1)} %copy-done.2, bf16[1536,384]{1,0:T(8,128)(2,1)S(1)} %copy-done.3), custom_call_target="tpu_custom_call" | custom-call | tf_op jit(solution)/shard_map/pallas_call | solution.py:445
  21.6 14.5 %shard_map.106 = (bf16[8,288,128]{2,1,0:T(8,128)(2,1)S(1)}, bf16[8,144,128]{2,1,0:T(8,128)(2,1)S(1)}, bf16[128,896]{1,0:T(8,128)(2,1)S(1)}) custom-call(bf16[6,288,128]{2,1,0:T(8,128)(2,1)S(1)} %get-tuple-element.26.refs_0_, bf16[6,144,128]{2,1,0:T(8,128)(2,1)S(1)} %get-tuple-element.27.refs_1_, bf16[4,128,896]{2,1,0:T(8,128)(2,1)S(1)} %bitcast.50), custom_call_target="tpu_custom_call" | custom-call | tf_op jit(solution)/shard_map/pallas_call | solution.py:200
  36.1 16.6 %shard_map.107 = (bf16[2304,128]{1,0:T(8,128)(2,1)S(1)}, bf16[2304,128]{1,0:T(8,128)(2,1)S(1)}, f32[1,2304]{1,0:T(1,128)S(1)}, f32[1,2304]{1,0:T(1,128)S(1)}, bf...) custom-call(bf16[2304,128]{1,0:T(8,128)(2,1)S(1)} %bitcast.54, ...), custom_call_target="tpu_custom_call" | custom-call | tf_op jit(solution)/shard_map/pallas_call | solution.py:377
  52.7 0.8 copy-done.10
  53.5 0.8 copy-done.12
  54.3 0.8 copy-done.14
  55.2 0.9 copy.22
  56.0 1.3 reshape.93.refs_0_
  57.4 1.3 copy-done.5
  58.6 0.9 copy-done.17
  59.6 0.7 shard_map.108
  60.2 14.7 %shard_map.109 = (bf16[4,72,1536]{2,1,0:T(8,128)(2,1)S(1)}, bf16[72,1536]{1,0:T(8,128)(2,1)S(1)}) custom-call(bf16[72,1536]{1,0:T(8,128)(2,1)S(1)} %reshape.93.refs_0_, bf16[4,72,1536]{2,1,0:T(8,128)(2,1)S(1)} %bitcast.52), custom_call_target="tpu_custom_call" | custom-call | tf_op jit(solution)/shard_map/pallas_call | solution.py:200
  75.0 0.0 copy-start.7
  75.0 0.9 copy-done.7
  75.9 0.7 copy-done.18
  76.6 1.4 reshape.96
  78.1 1.1 copy-done.8
  79.2 1.3 copy-done.6
  80.4 0.7 shard_map.110.refs_0_
  81.1 20.4 %shard_map.111 = (bf16[8,144,128]{2,1,0:T(8,128)(2,1)S(1)}, bf16[8,16,896]{2,1,0:T(8,128)(2,1)S(1)}) custom-call(bf16[6,144,128]{2,1,0:T(8,128)(2,1)S(1)} %shard_map.110.refs_0_, bf16[8,16,896]{2,1,0:T(8,128)(2,1)S(1)} %pad_bitcast_fusion.refs_1_), custom_call_target="tpu_custom_call" | custom-call | tf_op jit(solution)/shard_map/pallas_call | solution.py:200
  101.5 0.0 copy-start.4
  101.6 36.3 %shard_map.113 = (bf16[6,144,128]{2,1,0:T(8,128)(2,1)S(1)}, bf16[6,288,128]{2,1,0:T(8,128)(2,1)S(1)}, bf16[4,8,16,896]{3,2,1,0:T(8,128)(2,1)S(1)}) custom-call(bf16[8,144,128]{2,1,0:T(8,128)(2,1)S(1)} %get-tuple-element.42.refs_0_, bf16[8,288,128]{2,1,0:T(8,128)(2,1)S(1)} %bitcast.58, bf16[8,16,896]{2,1,0:T(8,128)(2,1)S(1)} %get-tuple-element.44.refs_2_), custom_call_target="tpu_custom_call" | custom-call | tf_op jit(solution)/shard_map/pallas_call | solution.py:200
  137.9 1.6 shard_map.114
  139.5 0.0 copy-start.20
  139.5 0.1 fusion.18
  139.6 1.2 copy-done.20
  140.8 0.4 fusion.11
  141.2 0.4 fusion.6
  141.7 12.9 %shard_map.115 = (bf16[72,1536]{1,0:T(8,128)(2,1)S(1)}, bf16[8,32,384]{2,1,0:T(8,128)(2,1)S(1)}) custom-call(bf16[4,72,1536]{2,1,0:T(8,128)(2,1)S(1)} %bitcast.51, bf16[8,32,384]{2,1,0:T(8,128)(2,1)S(1)} %bitcast.57), custom_call_target="tpu_custom_call" | custom-call | tf_op jit(solution)/shard_map/pallas_call | solution.py:200
  154.6 0.6 reduce_sum.30
  155.2 9.4 %shard_map.116 = bf16[4,72,1536]{2,1,0:T(8,128)(2,1)S(1)} custom-call(bf16[72,1536]{1,0:T(8,128)(2,1)S(1)} %get-tuple-element.49.refs_0_), custom_call_target="tpu_custom_call" | custom-call | tf_op jit(solution)/shard_map/pallas_call | solution.py:200
  164.6 0.5 fusion.3
  165.1 1.6 fusion.2
  (33 shorter events, 0.2 us)
Async XLA Ops:
  2.0 0.7 copy-start.19
  15.2 3.5 %copy-start.3 = (bf16[1536,384]{1,0:T(8,128)(2,1)S(1)}, bf16[1536,384]{1,0:T(8,128)(2,1)}, u32[]{:S(2)}) copy-start(bf16[1536,384]{1,0:T(8,128)(2,1)} %wv_ref.3) | copy-start | bytes 3538948
  16.9 1.8 %copy-start.1 = (bf16[1536,384]{1,0:T(8,128)(2,1)S(1)}, bf16[1536,384]{1,0:T(8,128)(2,1)}, u32[]{:S(2)}) copy-start(bf16[1536,384]{1,0:T(8,128)(2,1)} %wq_ref.3) | copy-start | bytes 3538948
  16.9 1.8 %copy-start.2 = (bf16[1536,384]{1,0:T(8,128)(2,1)S(1)}, bf16[1536,384]{1,0:T(8,128)(2,1)}, u32[]{:S(2)}) copy-start(bf16[1536,384]{1,0:T(8,128)(2,1)} %wk_ref.3) | copy-start | bytes 3538948
  18.6 1.2 copy-start
  52.7 0.8 copy-start.10
  53.5 0.8 copy-start.12
  54.3 0.8 copy-start.14
  55.2 0.9 copy-start.16
  57.4 1.3 copy-start.5
  58.6 0.9 copy-start.17
  75.0 0.9 copy-start.7
  75.9 0.7 copy-start.18
  78.0 1.2 copy-start.8
  79.1 1.3 copy-start.6
  80.4 21.1 %copy-start.11 = (bf16[8,288,128]{2,1,0:T(8,128)(2,1)S(1)}, bf16[8,288,128]{2,1,0:T(8,128)(2,1)}, u32[]{:S(2)}) copy-start(bf16[8,288,128]{2,1,0:T(8,128)(2,1)} %copy-done.10) | copy-start | bytes 1769476
  80.4 21.1 %copy-start.13 = (bf16[2304,128]{1,0:T(8,128)(2,1)S(1)}, bf16[2304,128]{1,0:T(8,128)(2,1)}, u32[]{:S(2)}) copy-start(bf16[2304,128]{1,0:T(8,128)(2,1)} %copy-done.12) | copy-start | bytes 1769476
  80.4 21.1 %copy-start.15 = (bf16[2304,128]{1,0:T(8,128)(2,1)S(1)}, bf16[2304,128]{1,0:T(8,128)(2,1)}, u32[]{:S(2)}) copy-start(bf16[2304,128]{1,0:T(8,128)(2,1)} %copy-done.14) | copy-start | bytes 1769476
  101.5 36.4 %copy-start.4 = (bf16[1536,384]{1,0:T(8,128)(2,1)S(1)}, bf16[1536,384]{1,0:T(8,128)(2,1)}, u32[]{:S(2)}) copy-start(bf16[1536,384]{1,0:T(8,128)(2,1)} %wv_ref.3) | copy-start | bytes 3538948
  139.5 1.3 copy-start.20
  141.6 22.9 %copy-start.21 = (f32[1536]{0:T(1024)S(1)}, f32[1536]{0:T(1024)}, u32[]{:S(2)}) copy-start(f32[1536]{0:T(1024)} %param.10) | copy-start | bytes 18436
  155.2 9.9 %copy-start.9 = (bf16[4,72,1536]{2,1,0:T(8,128)(2,1)S(1)}, bf16[4,72,1536]{2,1,0:T(8,128)(2,1)}, u32[]{:S(2)}) copy-start(bf16[4,72,1536]{2,1,0:T(8,128)(2,1)} %copy-done.7) | copy-start | bytes 2654212

commit v5 on v4

--- a/solution.py
+++ b/solution.py
@@ -436,8 +436,8 @@
 
 
 def tiling(total):
-    tile = next(size for size in (256, 128) if total % size == 0)
-    return tile, tile * (3 if total % (3 * tile) == 0 else 1)
+    tile = next(size for size in (384, 256, 128) if total % size == 0)
+    return tile, tile * (2 if total % (2 * tile) == 0 else 1)
 
 
 def plain_call(body, arrays, shapes, scratch=()):

time: 167 us -> 164 us (0.982)
  Pallas kernels: 141 us -> 139 us
    pallas_call x7, Pallas kernels: 120 us -> 117 us  [exchange(): pl.pallas_call(functools.partial(exchange_kernel, tuple(plan), heads, fir...]
where the time goes in v5:
time: 164 us
  Pallas kernels  139 us (85%)
  local copies, waits for them, and re-layouts  17.3 us (11%)
  matrix products  4.16 us (3%)
  other arithmetic  2.77 us (2%)
    pallas_call x7, Pallas kernels, exchange(): pl.pallas_call(functools.partial(exchange_kernel, tuple(plan), heads, fir...  117 us
    pallas_call x1, Pallas kernels, forward(): pl.pallas_call(functools.partial(forward_kernel, heads, tile, span), out_...  17.4 us
    unnamed x45, local copies, waits for them, and re-layouts  12.6 us
    pallas_call x5, Pallas kernels, plain_call(): pl.pallas_call(body, out_shape=[jax.ShapeDtypeStruct(*shape) for shape in...  4.78 us
    dot_general x2, matrix products, times_rows(): lax.dot_general(left, right, (((1,), (1,)), ((), ())), preferred_element_...  3.36 us

profile of v5, /device:TPU:0, one launch (start us, length us, event | category | flops | bytes accessed | tf_op | source)
XLA Modules:
  0.0 163.9 jit_solution(11324455407253416446)
XLA Ops:
  0.6 0.7 pad.12
  1.3 0.7 broadcast_in_dim.6.gain_ref
  2.0 0.7 copy-done.19
  2.7 12.0 %shard_map.105 = (bf16[8,32,384]{2,1,0:T(8,128)(2,1)S(1)}, s32[8,8,128]{2,1,0:T(8,128)S(1)}) custom-call(bf16[32,384]{1,0:T(8,128)(2,1)S(1)} %copy-done.19, s32[8,128]{1,0:T(8,128)S(1)} %broadcast_in_dim.7.refs_1_), custom_call_target="tpu_custom_call" | custom-call | tf_op jit(solution)/shard_map/pallas_call | solution.py:200
  14.8 0.1 reshape_squeeze.9
  14.9 0.1 broadcast_in_dim.8
  15.0 0.2 broadcast_in_dim_reshape.3.low_ref
  15.2 0.0 copy-start.3
  15.2 1.7 %convolution_convert_fusion = bf16[256,896]{1,0:T(8,128)(2,1)S(1)} fusion(bf16[256,384]{1,0:T(8,128)(2,1)S(1)} %bitcast.70, bf16[2,864,384]{2,1,0:T(8,128)(2,1)} %bitcast.62), kind=kOutput, calls=%fused_computation.11 | convolution fusion | flops 176390144 | bytes 1982464 | tf_op jit(solution)/shard_map/dot_general | solution.py:30
  16.9 0.0 copy-start.1
  16.9 0.0 copy-start.2
  16.9 1.7 %convolution_convert_fusion.1 = bf16[256,896]{1,0:T(8,128)(2,1)S(1)} fusion(bf16[256,384]{1,0:T(8,128)(2,1)S(1)} %bitcast.71, bf16[2,864,384]{2,1,0:T(8,128)(2,1)} %bitcast.63), kind=kOutput, calls=%fused_computation.12 | convolution fusion | flops 176390144 | bytes 1982464 | tf_op jit(solution)/shard_map/dot_general | solution.py:30
  18.6 0.0 copy-start
  18.6 0.1 pad_maximum_fusion
  18.8 1.1 copy-done
  19.8 1.8 %shard_map.104 = (bf16[6,288,128]{2,1,0:T(8,128)(2,1)S(1)}, bf16[6,144,128]{2,1,0:T(8,128)(2,1)S(1)}) custom-call(bf16[288,1536]{1,0:T(8,128)(2,1)S(1)} %copy-done, f32[1,1536]{1,0:T(1,128)S(1)} %broadcast_in_dim.6.gain_ref, bf16[1536,384]{1,0:T(8,128)(2,1)S(1)} %copy-done.1, bf16[1536,384]{1,0:T(8,128)(2,1)S(1)} %copy-done.2, bf16[1536,384]{1,0:T(8,128)(2,1)S(1)} %copy-done.3), custom_call_target="tpu_custom_call" | custom-call | tf_op jit(solution)/shard_map/pallas_call | solution.py:445
  21.6 14.5 %shard_map.106 = (bf16[8,288,128]{2,1,0:T(8,128)(2,1)S(1)}, bf16[8,144,128]{2,1,0:T(8,128)(2,1)S(1)}, bf16[128,896]{1,0:T(8,128)(2,1)S(1)}) custom-call(bf16[6,288,128]{2,1,0:T(8,128)(2,1)S(1)} %get-tuple-element.26.refs_0_, bf16[6,144,128]{2,1,0:T(8,128)(2,1)S(1)} %get-tuple-element.27.refs_1_, bf16[4,128,896]{2,1,0:T(8,128)(2,1)S(1)} %bitcast.50), custom_call_target="tpu_custom_call" | custom-call | tf_op jit(solution)/shard_map/pallas_call | solution.py:200
  36.1 17.4 %shard_map.107 = (bf16[2304,128]{1,0:T(8,128)(2,1)S(1)}, bf16[2304,128]{1,0:T(8,128)(2,1)S(1)}, f32[1,2304]{1,0:T(1,128)S(1)}, f32[1,2304]{1,0:T(1,128)S(1)}, bf...) custom-call(bf16[2304,128]{1,0:T(8,128)(2,1)S(1)} %bitcast.54, ...), custom_call_target="tpu_custom_call" | custom-call | tf_op jit(solution)/shard_map/pallas_call | solution.py:377
  53.5 0.8 copy-done.10
  54.3 0.8 copy-done.12
  55.1 0.8 copy-done.14
  56.0 0.9 copy.22
  56.8 1.3 reshape.93.refs_0_
  58.2 0.0 copy-start.5
  58.2 1.3 copy-done.5
  59.5 0.9 copy-done.17
  60.4 0.7 shard_map.108
  61.1 14.7 %shard_map.109 = (bf16[4,72,1536]{2,1,0:T(8,128)(2,1)S(1)}, bf16[72,1536]{1,0:T(8,128)(2,1)S(1)}) custom-call(bf16[72,1536]{1,0:T(8,128)(2,1)S(1)} %reshape.93.refs_0_, bf16[4,72,1536]{2,1,0:T(8,128)(2,1)S(1)} %bitcast.52), custom_call_target="tpu_custom_call" | custom-call | tf_op jit(solution)/shard_map/pallas_call | solution.py:200
  75.8 0.9 copy-done.7
  76.7 0.7 copy-done.18
  77.4 1.4 reshape.96
  78.8 0.0 copy-start.8
  78.9 1.1 copy-done.8
  79.9 1.3 copy-done.6
  81.2 0.7 shard_map.110.refs_0_
  81.9 17.9 %shard_map.111 = (bf16[8,144,128]{2,1,0:T(8,128)(2,1)S(1)}, bf16[8,16,896]{2,1,0:T(8,128)(2,1)S(1)}) custom-call(bf16[6,144,128]{2,1,0:T(8,128)(2,1)S(1)} %shard_map.110.refs_0_, bf16[8,16,896]{2,1,0:T(8,128)(2,1)S(1)} %pad_bitcast_fusion.refs_1_), custom_call_target="tpu_custom_call" | custom-call | tf_op jit(solution)/shard_map/pallas_call | solution.py:200
  99.9 35.3 %shard_map.113 = (bf16[6,144,128]{2,1,0:T(8,128)(2,1)S(1)}, bf16[6,288,128]{2,1,0:T(8,128)(2,1)S(1)}, bf16[4,8,16,896]{3,2,1,0:T(8,128)(2,1)S(1)}) custom-call(bf16[8,144,128]{2,1,0:T(8,128)(2,1)S(1)} %get-tuple-element.42.refs_0_, bf16[8,288,128]{2,1,0:T(8,128)(2,1)S(1)} %bitcast.58, bf16[8,16,896]{2,1,0:T(8,128)(2,1)S(1)} %get-tuple-element.44.refs_2_), custom_call_target="tpu_custom_call" | custom-call | tf_op jit(solution)/shard_map/pallas_call | solution.py:200
  135.2 1.6 shard_map.114
  136.7 0.0 copy-start.20
  136.8 0.1 fusion.18
  136.9 1.2 copy-done.20
  138.1 0.4 fusion.11
  138.5 0.4 fusion.6
  138.9 12.9 %shard_map.115 = (bf16[72,1536]{1,0:T(8,128)(2,1)S(1)}, bf16[8,32,384]{2,1,0:T(8,128)(2,1)S(1)}) custom-call(bf16[4,72,1536]{2,1,0:T(8,128)(2,1)S(1)} %bitcast.51, bf16[8,32,384]{2,1,0:T(8,128)(2,1)S(1)} %bitcast.57), custom_call_target="tpu_custom_call" | custom-call | tf_op jit(solution)/shard_map/pallas_call | solution.py:200
  151.8 0.6 reduce_sum.30
  152.4 9.4 %shard_map.116 = bf16[4,72,1536]{2,1,0:T(8,128)(2,1)S(1)} custom-call(bf16[72,1536]{1,0:T(8,128)(2,1)S(1)} %get-tuple-element.49.refs_0_), custom_call_target="tpu_custom_call" | custom-call | tf_op jit(solution)/shard_map/pallas_call | solution.py:200
  161.8 0.5 fusion.3
  162.3 1.6 fusion.2
  (33 shorter events, 0.2 us)
Async XLA Ops:
  2.0 0.7 copy-start.19
  15.2 3.5 %copy-start.3 = (bf16[1536,384]{1,0:T(8,128)(2,1)S(1)}, bf16[1536,384]{1,0:T(8,128)(2,1)}, u32[]{:S(2)}) copy-start(bf16[1536,384]{1,0:T(8,128)(2,1)} %wv_ref.3) | copy-start | bytes 3538948
  16.9 1.8 %copy-start.1 = (bf16[1536,384]{1,0:T(8,128)(2,1)S(1)}, bf16[1536,384]{1,0:T(8,128)(2,1)}, u32[]{:S(2)}) copy-start(bf16[1536,384]{1,0:T(8,128)(2,1)} %wq_ref.3) | copy-start | bytes 3538948
  16.9 1.8 %copy-start.2 = (bf16[1536,384]{1,0:T(8,128)(2,1)S(1)}, bf16[1536,384]{1,0:T(8,128)(2,1)}, u32[]{:S(2)}) copy-start(bf16[1536,384]{1,0:T(8,128)(2,1)} %wk_ref.3) | copy-start | bytes 3538948
  18.6 1.2 copy-start
  53.5 0.8 copy-start.10
  54.3 0.8 copy-start.12
  55.1 0.8 copy-start.14
  56.0 0.9 copy-start.16
  58.2 1.3 copy-start.5
  59.4 0.9 copy-start.17
  75.7 0.9 copy-start.7
  76.7 0.7 copy-start.18
  78.8 1.2 copy-start.8
  79.9 1.3 copy-start.6
  81.2 18.6 %copy-start.11 = (bf16[8,288,128]{2,1,0:T(8,128)(2,1)S(1)}, bf16[8,288,128]{2,1,0:T(8,128)(2,1)}, u32[]{:S(2)}) copy-start(bf16[8,288,128]{2,1,0:T(8,128)(2,1)} %copy-done.10) | copy-start | bytes 1769476
  81.2 18.6 %copy-start.13 = (bf16[2304,128]{1,0:T(8,128)(2,1)S(1)}, bf16[2304,128]{1,0:T(8,128)(2,1)}, u32[]{:S(2)}) copy-start(bf16[2304,128]{1,0:T(8,128)(2,1)} %copy-done.12) | copy-start | bytes 1769476
  81.2 18.6 %copy-start.15 = (bf16[2304,128]{1,0:T(8,128)(2,1)S(1)}, bf16[2304,128]{1,0:T(8,128)(2,1)}, u32[]{:S(2)}) copy-start(bf16[2304,128]{1,0:T(8,128)(2,1)} %copy-done.14) | copy-start | bytes 1769476
  99.8 35.3 %copy-start.4 = (bf16[1536,384]{1,0:T(8,128)(2,1)S(1)}, bf16[1536,384]{1,0:T(8,128)(2,1)}, u32[]{:S(2)}) copy-start(bf16[1536,384]{1,0:T(8,128)(2,1)} %wv_ref.3) | copy-start | bytes 3538948
  136.7 1.3 copy-start.20
  138.9 22.9 %copy-start.21 = (f32[1536]{0:T(1024)S(1)}, f32[1536]{0:T(1024)}, u32[]{:S(2)}) copy-start(f32[1536]{0:T(1024)} %param.10) | copy-start | bytes 18436
  152.4 9.9 %copy-start.9 = (bf16[4,72,1536]{2,1,0:T(8,128)(2,1)S(1)}, bf16[4,72,1536]{2,1,0:T(8,128)(2,1)}, u32[]{:S(2)}) copy-start(bf16[4,72,1536]{2,1,0:T(8,128)(2,1)} %copy-done.7) | copy-start | bytes 2654212
